TPU v7x, 32 devices: a whole 2x2x4 slice. The times are simulated.
32 devices in a mesh: parts: 2 (over y), pool: 4 (over z), tp: 4 (over x, core).
Axes of the slice: x: 2, y: 2, z: 4, core: 2. Of those that a mesh axis runs over, the one named last changes fastest.
Arguments:
- queries: bfloat16 [4096, 8192], P(('parts', 'pool'), 'tp'), parts along dimension 0, may hold values from -400 to 400
- suffix_kv: bfloat16 [2, 8, 4096, 128], P(None, 'tp', ('parts', 'pool')), parts along dimension 2, may hold values from -12 to 12
- pool_kv: bfloat16 [2, 8, 64, 128, 128], P(None, 'tp', ('parts', 'pool')), parts along dimension 2, may hold values from -6 to 6
- prefix_pages: int32 [8], P('parts'), parts along dimension 0, may hold values from 1 to 4, as said below
- owner_start: int32 [8], P('parts'), parts along dimension 0, may hold values from 0 to 3
- page_slot: int32 [8, 4, 2], P('parts'), parts along dimension 0, may hold values from 0 to 7, as said below
Outputs:
- attention: bfloat16 [4096, 8192], P(('parts', 'pool'), 'tp'), parts along dimension 0
- new_pool: bfloat16 [2, 8, 64, 128, 128], P(None, 'tp', ('parts', 'pool')), parts along dimension 2
There are 2 independent parts, one for each index of `parts`. A program takes and returns all parts, laid end to end along the dimension named above; each array names one. Nothing has to cross between parts.
Inputs may be any that keep to these rules, and one draw needn't show every extreme that they name: For each owner o, the entries page_slot[:, o, :] name each of its 8 slots exactly once. `prefix_pages`: among the 4 requests of one serving group, at least one has exactly 4 prefix pages.
All inputs are finite; a program needn't handle non-finite values.
Results may differ from a plain program's by a relative error of at most 0.0035.
Values may be sent and summed in bfloat16 or wider, within the bound.
No kernel may reach another device: no remote copies, remote signals or barrier semaphores. Data moves between devices by JAX's collectives and lax.ppermute only.
A program may use at most 128 MiB of HBM per device.

v0:
```python
import functools
import math

import jax
import jax.numpy as jnp
from jax import lax
from jax.experimental import pallas as pl
from jax.experimental.pallas import tpu as pltpu
from jax.sharding import PartitionSpec as P

HBM = pl.BlockSpec(memory_space=pl.ANY)
VMEM = pl.BlockSpec(memory_space=pltpu.VMEM)
SMEM = pl.BlockSpec(memory_space=pltpu.SMEM)
TILE = 256


def partner(index, step, groups):
    if groups & (groups - 1):
        return (index + step) % groups, (index + groups - step) % groups
    return index ^ step, index ^ step


def fetch_kernel(slots_ref, pool_ref, *rest):
    *sends, own_ref, sems = rest
    groups = slots_ref.shape[2]
    levels = sends[0].shape[0]
    me = lax.axis_index("pool")
    copies = []
    for step in range(groups - 1, 0, -1):
        dest = partner(me, step, groups)[0]
        for level in range(levels):
            slot = slots_ref[dest, level, me]
            copies.append(
                pltpu.make_async_copy(
                    pool_ref.at[:, :, slot], sends[step - 1].at[level], sems.at[step, level]
                )
            )
    for copy in copies:
        copy.start()
    for level in range(levels):
        own_ref[level] = slots_ref[me, level, me]
    for copy in copies:
        copy.wait()


def place_kernel(pages, length_ref, start_ref, slots_ref, *rest):
    backs, new_ref, sems = rest[:-4], rest[-2], rest[-1]
    _, levels, groups = slots_ref.shape
    me = lax.axis_index("pool")

    def each(act):
        for step in range(groups):
            request = partner(me, step, groups)[1]
            length = length_ref[request]
            first = lax.rem(start_ref[request] + length, groups)
            offset = lax.rem(me + groups - first, groups)

            @pl.when(offset < pages)
            def _():
                level = jnp.minimum(lax.div(length + offset, groups), levels - 1)
                slot = slots_ref[request, level, me]
                act(
                    pltpu.make_async_copy(backs[step], new_ref.at[:, :, slot], sems.at[step])
                )

    each(lambda copy: copy.start())
    each(lambda copy: copy.wait())


dot = functools.partial(lax.dot_general, preferred_element_type=jnp.float32)
ACROSS = (((1,), (1,)), ((), ()))
ALONG = (((1,), (0,)), ((), ()))


def staggered(items, scores_of, finish):
    ahead = scores_of(items[0])
    for place, item in enumerate(items):
        scores = ahead
        if place + 1 < len(items):
            ahead = scores_of(items[place + 1])
        finish(item, scores)


def suffix_kernel(
    scale, per_step, length_ref, start_ref, own_ref, query_ref, suffix_ref, pool_ref, *rest
):
    sum_ref, top_ref, new_ref, page_ref, *back_refs, values, sem = rest
    groups = len(back_refs)
    page_len, head_dim = pool_ref.shape[3:]
    suffix = query_ref.shape[0]
    pages = suffix // page_len
    head, step = pl.program_id(0), pl.program_id(1)
    copy = pltpu.make_async_copy(pool_ref, new_ref.at[:, pl.ds(head, 1)], sem)

    @pl.when(step == 0)
    def _():
        copy.start()
        values[:, pl.ds(0, head_dim)] = suffix_ref[1, 0]
        values[:, pl.ds(head_dim, head_dim)] = jnp.ones((suffix, head_dim), values.dtype)
        me = lax.axis_index("pool")
        first = lax.rem(start_ref[me] + length_ref[me], groups)
        for turn in range(groups):
            offset = lax.rem(partner(me, turn, groups)[0] + groups - first, groups)
            row = pl.multiple_of(jnp.minimum(offset, pages - 1) * page_len, page_len)
            for side in range(2):
                back_refs[turn][side, 0] = suffix_ref[side, 0, pl.ds(row, page_len), :]
        for level in range(page_ref.shape[0]):
            for side in range(2):
                page_ref[level, side, 0] = pool_ref[side, 0, own_ref[level]]

    tile = min(TILE, suffix)
    seen = lax.broadcasted_iota(jnp.int32, (tile, tile), 1) <= lax.broadcasted_iota(
        jnp.int32, (tile, tile), 0
    )

    def scores_of(item):
        column, row = item
        query = query_ref[pl.ds(row, tile), pl.ds(column * head_dim, head_dim)]
        score = dot(query, suffix_ref[0, 0, pl.ds(row, tile), :], ACROSS)
        parts = [(jnp.where(seen, score, -jnp.inf), pl.ds(row, tile))]
        if row:
            early = pl.ds(0, row)
            parts.append((dot(query, suffix_ref[0, 0, early, :], ACROSS), early))
        return parts

    def finish(item, parts):
        column, row = item
        top = functools.reduce(
            jnp.maximum, [jnp.max(score, axis=1, keepdims=True) for score, _ in parts]
        )
        mixed = functools.reduce(
            jnp.add,
            [
                dot(jnp.exp2((score - top) * scale).astype(jnp.bfloat16), values[keys, :], ALONG)
                for score, keys in parts
            ],
        )
        rows = pl.ds(row, tile)
        sum_ref[rows, pl.ds(column * 2 * head_dim, 2 * head_dim)] = mixed
        top_ref[rows, pl.ds(column * head_dim, head_dim)] = jnp.broadcast_to(
            top, (tile, head_dim)
        )

    staggered(
        [(column, row) for column in range(per_step) for row in range(0, suffix, tile)],
        scores_of,
        finish,
    )

    @pl.when(step == pl.num_programs(1) - 1)
    def _():
        copy.wait()


def prefix_kernel(
    scale, per_step, length_ref, start_ref, query_ref, suffix_ref, sum_ref, top_ref, *rest
):
    *page_refs, out_ref, keys, values = rest
    groups = len(page_refs)
    levels, _, _, page_len, head_dim = page_refs[0].shape
    suffix = query_ref.shape[0]

    @pl.when(pl.program_id(1) == 0)
    def _():
        me = lax.axis_index("pool")
        length, first = length_ref[me], start_ref[me]
        for turn in range(groups):
            owner = partner(me, turn, groups)[1]
            for level in range(levels):
                rows = pl.ds((turn * levels + level) * page_len, page_len)
                seen = level * groups + lax.rem(owner + groups - first, groups) < length

                @pl.when(seen)
                def _():
                    keys[rows, :] = page_refs[turn][level, 0, 0]
                    values[rows, pl.ds(0, head_dim)] = page_refs[turn][level, 1, 0]
                    values[rows, pl.ds(head_dim, head_dim)] = jnp.ones(
                        (page_len, head_dim), values.dtype
                    )

                @pl.when(jnp.logical_not(seen))
                def _():
                    keys[rows, :] = jnp.broadcast_to(
                        suffix_ref[0, 0, pl.ds(0, 1), :], (page_len, head_dim)
                    )
                    values[rows, :] = jnp.zeros((page_len, 2 * head_dim), values.dtype)

    tile = min(TILE, suffix)

    def scores_of(item):
        column, row = item
        query = query_ref[pl.ds(row, tile), pl.ds(column * head_dim, head_dim)]
        return dot(query, keys[...], ACROSS)

    def finish(item, score):
        column, row = item
        rows = pl.ds(row, tile)
        lanes = pl.ds(column * head_dim, head_dim)
        before = top_ref[rows, lanes]
        top = jnp.maximum(before, jnp.max(score, axis=1, keepdims=True))
        factor = jnp.exp2((before - top) * scale)
        weight = jnp.concatenate(
            [
                jnp.exp2((score[:, start : start + head_dim] - top) * scale).astype(jnp.bfloat16)
                for start in range(0, score.shape[1], head_dim)
            ],
            axis=1,
        )
        mixed = dot(weight, values[...], ALONG)
        sums = sum_ref[rows, pl.ds(column * 2 * head_dim, head_dim)]
        count = sum_ref[rows, pl.ds(column * 2 * head_dim + head_dim, head_dim)]
        total = mixed[:, head_dim:] + count * factor
        out_ref[rows, lanes] = ((mixed[:, :head_dim] + sums * factor) / total).astype(
            out_ref.dtype
        )

    staggered(
        [(column, row) for column in range(per_step) for row in range(0, suffix, tile)],
        scores_of,
        finish,
    )


def body(queries, suffix_kv, pool_kv, prefix_pages, owner_start, page_slot):
    _, heads, slots, page_len, head_dim = pool_kv.shape
    _, groups, levels = page_slot.shape
    suffix = queries.shape[0]
    per_kv = queries.shape[1] // (heads * head_dim)
    pages = suffix // page_len
    fetched = -(-(levels * groups - pages) // groups)
    page = (2, heads, page_len, head_dim)
    slot_of = jnp.swapaxes(page_slot, 1, 2)
    dtype = pool_kv.dtype

    def exchange(sends):
        arrived = [None] * (groups - 1)
        for step in range(groups - 1, 0, -1):
            pairs = [(index, partner(index, step, groups)[0]) for index in range(groups)]
            arrived[step - 1] = lax.ppermute(sends[step - 1], "pool", pairs)
        return arrived

    *sends, own_slots = pl.pallas_call(
        fetch_kernel,
        out_shape=[pltpu.VMEM((fetched,) + page, dtype)] * (groups - 1)
        + [jax.ShapeDtypeStruct((fetched,), jnp.int32)],
        in_specs=[SMEM, HBM],
        out_specs=[VMEM] * (groups - 1) + [SMEM],
        scratch_shapes=[pltpu.SemaphoreType.DMA((groups, fetched))],
        name="gather_pages",
    )(slot_of, pool_kv)
    received = exchange(sends)

    per_step = math.gcd(per_kv, 4)
    steps = per_kv // per_step
    scale = math.log2(math.e) / math.sqrt(head_dim)
    total = fetched * groups * page_len
    params = pltpu.CompilerParams(vmem_limit_bytes=60 * 1024 * 1024)
    columns = pl.BlockSpec((suffix, per_step * head_dim), lambda h, s: (0, h * steps + s))
    doubled = pl.BlockSpec((suffix, 2 * per_step * head_dim), lambda h, s: (0, h * steps + s))
    pages_of = pl.BlockSpec((fetched, 2, 1, page_len, head_dim), lambda h, s: (0, 0, h, 0, 0))

    def cost(keys):
        cells = heads * per_kv * suffix * keys
        return pl.CostEstimate(
            flops=6 * cells * head_dim, bytes_accessed=8 * queries.size, transcendentals=cells
        )

    sums, tops, new_pool, own_pages, own_back, *back_sends = pl.pallas_call(
        functools.partial(suffix_kernel, scale, per_step),
        grid=(heads, steps),
        out_shape=[
            jax.ShapeDtypeStruct((suffix, 2 * queries.shape[1]), jnp.float32),
            jax.ShapeDtypeStruct(queries.shape, jnp.float32),
            jax.ShapeDtypeStruct(pool_kv.shape, dtype),
            jax.ShapeDtypeStruct((fetched,) + page, dtype),
        ]
        + [jax.ShapeDtypeStruct(page, dtype)] * groups,
        in_specs=[
            SMEM,
            SMEM,
            SMEM,
            columns,
            pl.BlockSpec((2, 1, suffix, head_dim), lambda h, s: (0, h, 0, 0)),
            pl.BlockSpec((2, 1, slots, page_len, head_dim), lambda h, s: (0, h, 0, 0, 0)),
        ],
        out_specs=[doubled, columns, HBM, pages_of]
        + [pl.BlockSpec((2, 1, page_len, head_dim), lambda h, s: (0, h, 0, 0))] * groups,
        scratch_shapes=[
            pltpu.VMEM((suffix, 2 * head_dim), dtype),
            pltpu.SemaphoreType.DMA(()),
        ],
        compiler_params=params,
        cost_estimate=cost(suffix),
        name="attend_suffix",
    )(prefix_pages, owner_start, own_slots, queries, suffix_kv, pool_kv)
    returned = exchange(back_sends)

    result = pl.pallas_call(
        functools.partial(prefix_kernel, scale, per_step),
        grid=(heads, steps),
        out_shape=jax.ShapeDtypeStruct(queries.shape, dtype),
        in_specs=[
            SMEM,
            SMEM,
            columns,
            pl.BlockSpec((1, 1, page_len, head_dim), lambda h, s: (0, h, 0, 0)),
            doubled,
            columns,
        ]
        + [pages_of] * groups,
        out_specs=columns,
        scratch_shapes=[
            pltpu.VMEM((total, head_dim), dtype),
            pltpu.VMEM((total, 2 * head_dim), dtype),
        ],
        compiler_params=params,
        cost_estimate=cost(total),
        name="attend_prefix",
    )(prefix_pages, owner_start, queries, suffix_kv, sums, tops, own_pages, *received)

    new_pool = pl.pallas_call(
        functools.partial(place_kernel, pages),
        out_shape=jax.ShapeDtypeStruct(pool_kv.shape, dtype),
        in_specs=[SMEM, SMEM, SMEM] + [VMEM] * groups + [HBM, HBM],
        out_specs=HBM,
        input_output_aliases={4 + groups: 0},
        scratch_shapes=[pltpu.SemaphoreType.DMA((groups,))],
        compiler_params=params,
        name="place_pages",
    )(prefix_pages, owner_start, slot_of, own_back, *returned, result, new_pool)
    return (result, new_pool)


def solution(mesh):
    in_specs = (
        P(("parts", "pool"), "tp"),
        P(None, "tp", ("parts", "pool"), None),
        P(None, "tp", ("parts", "pool"), None, None),
        P("parts"),
        P("parts"),
        P("parts", None, None),
    )
    out_specs = (P(("parts", "pool"), "tp"), P(None, "tp", ("parts", "pool"), None, None))
    return jax.shard_map(body, mesh=mesh, in_specs=in_specs, out_specs=out_specs, check_vma=False)
```

profile of v0, /device:TPU:0, one launch (start us, length us, event | category | flops | bytes accessed | tf_op | source)
XLA Modules:
  0.0 37.0 jit_solution(13384091524691155456)
XLA Ops:
  0.6 2.3 %gather_pages.1 = (bf16[1,2,2,128,128]{4,3,2,1,0:T(8,128)(2,1)S(1)}, bf16[1,2,2,128,128]{4,3,2,1,0:T(8,128)(2,1)S(1)}, bf16[1,2,2,128,128]{4,3,2,1,0:T(8,128)(2,1)S(1)}, s32[1]{0:T(128)}) custom-call(s32[4,2,4]{2,1,0:T(2,128)} %bitcast.1, bf16[2,2,8,128,128]{4,3,2,1,0:T(8,128)(2,1)} %pool_ref.3), custom_call_target="tpu_custom_call" | custom-call | tf_op jit(solution)/shard_map/gather_pages/pallas_call | solution.py:242
  3.0 3.1 %collective-permute-start = (bf16[1,2,2,128,128]{4,3,2,1,0:T(8,128)(2,1)S(1)}, bf16[1,2,2,128,128]{4,3,2,1,0:T(8,128)(2,1)S(1)}, u32[]{:S(2)}, u32[]{:S(2)}) collective-permute-start(bf16[1,2,2,128,128]{4,3,2,1,0:T(8,128)(2,1)S(1)} %get-tuple-element.18), channel_id=1, source_target_pairs={{0,4},{4,0},{8,12},{12,8},{1,5},{5,1},{9,13},{13,9},{2,6},{6,2},{1... | collective-permute-start | bytes 393224 | tf_op jit(solution)/shard_map/ppermute | solution.py:239
  6.0 2.6 %collective-permute-start.1 = (bf16[1,2,2,128,128]{4,3,2,1,0:T(8,128)(2,1)S(1)}, bf16[1,2,2,128,128]{4,3,2,1,0:T(8,128)(2,1)S(1)}, u32[]{:S(2)}, u32[]{:S(2)}) collective-permute-start(bf16[1,2,2,128,128]{4,3,2,1,0:T(8,128)(2,1)S(1)} %get-tuple-element.19), channel_id=1, source_target_pairs={{0,8},{4,12},{8,0},{12,4},{1,9},{5,13},{9,1},{13,5},{2,10},{6,14},... | collective-permute-start | bytes 393224 | tf_op jit(solution)/shard_map/ppermute | solution.py:239
  8.6 0.0 collective-permute-start.2
  8.6 10.0 %attend_suffix.1 = (f32[512,4096]{1,0:T(8,128)}, f32[512,2048]{1,0:T(8,128)}, bf16[2,2,8,128,128]{4,3,2,1,0:T(8,128)(2,1)}, bf16[1,2,2,128,128]{4,3,2,1,0:T(8,12...) custom-call(s32[4]{0:T(128)} %length_ref.5, ...), custom_call_target="tpu_custom_call" | custom-call | flops 3221225472 | bytes 8388608 | tf_op jit(solution)/shard_map/attend_suffix/pallas_call | solution.py:268
  18.6 1.0 %collective-permute-start.3 = (bf16[2,2,128,128]{3,2,1,0:T(8,128)(2,1)}, bf16[2,2,128,128]{3,2,1,0:T(8,128)(2,1)S(1)}, u32[]{:S(2)}, u32[]{:S(2)}) collective-permute-start(bf16[2,2,128,128]{3,2,1,0:T(8,128)(2,1)} %get-tuple-element.22), channel_id=1, source_target_pairs={{0,4},{4,0},{8,12},{12,8},{1,5},{5,1},{9,13},{13,9},{2,6},{6,2},{1... | collective-permute-start | bytes 393224 | tf_op jit(solution)/shard_map/ppermute | solution.py:239
  19.6 3.5 %collective-permute-start.4 = (bf16[2,2,128,128]{3,2,1,0:T(8,128)(2,1)}, bf16[2,2,128,128]{3,2,1,0:T(8,128)(2,1)S(1)}, u32[]{:S(2)}, u32[]{:S(2)}) collective-permute-start(bf16[2,2,128,128]{3,2,1,0:T(8,128)(2,1)} %get-tuple-element.23), channel_id=1, source_target_pairs={{0,8},{4,12},{8,0},{12,4},{1,9},{5,13},{9,1},{13,5},{2,10},{6,14},... | collective-permute-start | bytes 393224 | tf_op jit(solution)/shard_map/ppermute | solution.py:239
  23.1 0.0 collective-permute-done.rest_1_
  23.1 0.0 copy-start
  23.1 0.0 collective-permute-start.5
  23.1 0.0 collective-permute-done.1.rest_2_
  23.1 0.0 copy-start.1
  23.1 0.0 collective-permute-done.2.rest_3_
  23.1 0.0 copy-start.2
  23.1 0.6 %copy-done = bf16[1,2,2,128,128]{4,3,2,1,0:T(8,128)(2,1)} copy-done((bf16[1,2,2,128,128]{4,3,2,1,0:T(8,128)(2,1)}, bf16[1,2,2,128,128]{4,3,2,1,0:T(8,128)(2,1)S(1)}, u32[]{:S(2)}) %copy-start) | copy-done | bytes 131096
  23.7 0.1 copy-done.1
  23.8 0.1 copy-done.2
  23.8 10.4 %attend_prefix.1.rest_4_ = bf16[512,2048]{1,0:T(8,128)(2,1)} custom-call(s32[4]{0:T(128)} %length_ref.5, s32[4]{0:T(128)} %start_ref.5, bf16[512,2048]{1,0:T(8,128)(2,1)} %query_ref.3, bf16[2,2,512,128]{3,2,1,0:T(8,128)(2,1)} %suffix_ref.3, f32[512,4096]{1,0:T(8,128)} %get-tuple-element.15.sum_ref, f32[512,2048]{1,0:T(8,128)} %get-tuple-element.16.top_ref, ...), custom_call_target="tpu_custom_call" | custom-call | flops 3221225472 | bytes 8388608 | tf_op jit(solution)/shard_map/attend_prefix/pallas_call | solution.py:298
  34.3 0.0 collective-permute-done.3.rest_1_
  34.3 0.0 copy-start.3
  34.3 0.0 collective-permute-done.4.rest_2_
  34.3 0.0 copy-start.4
  34.3 0.0 collective-permute-done.5.rest_3_
  34.3 0.0 copy-start.5
  34.3 0.6 %copy-done.3 = bf16[2,2,128,128]{3,2,1,0:T(8,128)(2,1)} copy-done((bf16[2,2,128,128]{3,2,1,0:T(8,128)(2,1)}, bf16[2,2,128,128]{3,2,1,0:T(8,128)(2,1)S(1)}, u32[]{:S(2)}) %copy-start.3) | copy-done | bytes 131096
  34.9 0.0 copy-done.4
  35.0 0.0 copy-done.5
  35.0 2.0 %place_pages.1 = bf16[2,2,8,128,128]{4,3,2,1,0:T(8,128)(2,1)} custom-call(s32[4]{0:T(128)} %length_ref.5, s32[4]{0:T(128)} %start_ref.5, s32[4,2,4]{2,1,0:T(2,128)} %bitcast.2, bf16[2,2,128,128]{3,2,1,0:T(8,128)(2,1)} %get-tuple-element.21.rest_0_, bf16[2,2,128,128]{3,2,1,0:T(8,128)(2,1)} %copy-done.3, ...), custom_call_target="tpu_custom_call", output_to_operand_aliasing={{}: (8, {})} | custom-call | tf_op jit(solution)/shard_map/place_pages/pallas_call | solution.py:321
Async XLA Ops:
  3.0 20.1 %collective-permute-start = (bf16[1,2,2,128,128]{4,3,2,1,0:T(8,128)(2,1)S(1)}, bf16[1,2,2,128,128]{4,3,2,1,0:T(8,128)(2,1)S(1)}, u32[]{:S(2)}, u32[]{:S(2)}) collective-permute-start(bf16[1,2,2,128,128]{4,3,2,1,0:T(8,128)(2,1)S(1)} %get-tuple-element.18), channel_id=1, source_target_pairs={{0,4},{4,0},{8,12},{12,8},{1,5},{5,1},{9,13},{13,9},{2,6},{6,2},{1... | collective-permute-start | bytes 393224 | tf_op jit(solution)/shard_map/ppermute | solution.py:239
  6.0 17.0 %collective-permute-start.1 = (bf16[1,2,2,128,128]{4,3,2,1,0:T(8,128)(2,1)S(1)}, bf16[1,2,2,128,128]{4,3,2,1,0:T(8,128)(2,1)S(1)}, u32[]{:S(2)}, u32[]{:S(2)}) collective-permute-start(bf16[1,2,2,128,128]{4,3,2,1,0:T(8,128)(2,1)S(1)} %get-tuple-element.19), channel_id=1, source_target_pairs={{0,8},{4,12},{8,0},{12,4},{1,9},{5,13},{9,1},{13,5},{2,10},{6,14},... | collective-permute-start | bytes 393224 | tf_op jit(solution)/shard_map/ppermute | solution.py:239
  8.6 14.4 %collective-permute-start.2 = (bf16[1,2,2,128,128]{4,3,2,1,0:T(8,128)(2,1)S(1)}, bf16[1,2,2,128,128]{4,3,2,1,0:T(8,128)(2,1)S(1)}, u32[]{:S(2)}, u32[]{:S(2)}) collective-permute-start(bf16[1,2,2,128,128]{4,3,2,1,0:T(8,128)(2,1)S(1)} %get-tuple-element.20), channel_id=1, source_target_pairs={{0,12},{4,8},{8,4},{12,0},{1,13},{5,9},{9,5},{13,1},{2,14},{6,10},... | collective-permute-start | bytes 393224 | tf_op jit(solution)/shard_map/ppermute | solution.py:239
  18.6 15.6 %collective-permute-start.3 = (bf16[2,2,128,128]{3,2,1,0:T(8,128)(2,1)}, bf16[2,2,128,128]{3,2,1,0:T(8,128)(2,1)S(1)}, u32[]{:S(2)}, u32[]{:S(2)}) collective-permute-start(bf16[2,2,128,128]{3,2,1,0:T(8,128)(2,1)} %get-tuple-element.22), channel_id=1, source_target_pairs={{0,4},{4,0},{8,12},{12,8},{1,5},{5,1},{9,13},{13,9},{2,6},{6,2},{1... | collective-permute-start | bytes 393224 | tf_op jit(solution)/shard_map/ppermute | solution.py:239
  19.6 14.7 %collective-permute-start.4 = (bf16[2,2,128,128]{3,2,1,0:T(8,128)(2,1)}, bf16[2,2,128,128]{3,2,1,0:T(8,128)(2,1)S(1)}, u32[]{:S(2)}, u32[]{:S(2)}) collective-permute-start(bf16[2,2,128,128]{3,2,1,0:T(8,128)(2,1)} %get-tuple-element.23), channel_id=1, source_target_pairs={{0,8},{4,12},{8,0},{12,4},{1,9},{5,13},{9,1},{13,5},{2,10},{6,14},... | collective-permute-start | bytes 393224 | tf_op jit(solution)/shard_map/ppermute | solution.py:239
  23.1 0.6 %copy-start = (bf16[1,2,2,128,128]{4,3,2,1,0:T(8,128)(2,1)}, bf16[1,2,2,128,128]{4,3,2,1,0:T(8,128)(2,1)S(1)}, u32[]{:S(2)}) copy-start(bf16[1,2,2,128,128]{4,3,2,1,0:T(8,128)(2,1)S(1)} %collective-permute-done.rest_1_) | copy-start | bytes 393220
  23.1 11.2 %collective-permute-start.5 = (bf16[2,2,128,128]{3,2,1,0:T(8,128)(2,1)}, bf16[2,2,128,128]{3,2,1,0:T(8,128)(2,1)S(1)}, u32[]{:S(2)}, u32[]{:S(2)}) collective-permute-start(bf16[2,2,128,128]{3,2,1,0:T(8,128)(2,1)} %get-tuple-element.24), channel_id=1, source_target_pairs={{0,12},{4,8},{8,4},{12,0},{1,13},{5,9},{9,5},{13,1},{2,14},{6,10},... | collective-permute-start | bytes 393224 | tf_op jit(solution)/shard_map/ppermute | solution.py:239
  23.1 0.7 %copy-start.1 = (bf16[1,2,2,128,128]{4,3,2,1,0:T(8,128)(2,1)}, bf16[1,2,2,128,128]{4,3,2,1,0:T(8,128)(2,1)S(1)}, u32[]{:S(2)}) copy-start(bf16[1,2,2,128,128]{4,3,2,1,0:T(8,128)(2,1)S(1)} %collective-permute-done.1.rest_2_) | copy-start | bytes 393220
  23.1 0.7 %copy-start.2 = (bf16[1,2,2,128,128]{4,3,2,1,0:T(8,128)(2,1)}, bf16[1,2,2,128,128]{4,3,2,1,0:T(8,128)(2,1)S(1)}, u32[]{:S(2)}) copy-start(bf16[1,2,2,128,128]{4,3,2,1,0:T(8,128)(2,1)S(1)} %collective-permute-done.2.rest_3_) | copy-start | bytes 393220
  34.3 0.7 %copy-start.3 = (bf16[2,2,128,128]{3,2,1,0:T(8,128)(2,1)}, bf16[2,2,128,128]{3,2,1,0:T(8,128)(2,1)S(1)}, u32[]{:S(2)}) copy-start(bf16[2,2,128,128]{3,2,1,0:T(8,128)(2,1)S(1)} %collective-permute-done.3.rest_1_) | copy-start | bytes 393220
  34.3 0.7 %copy-start.4 = (bf16[2,2,128,128]{3,2,1,0:T(8,128)(2,1)}, bf16[2,2,128,128]{3,2,1,0:T(8,128)(2,1)S(1)}, u32[]{:S(2)}) copy-start(bf16[2,2,128,128]{3,2,1,0:T(8,128)(2,1)S(1)} %collective-permute-done.4.rest_2_) | copy-start | bytes 393220
  34.3 0.7 %copy-start.5 = (bf16[2,2,128,128]{3,2,1,0:T(8,128)(2,1)}, bf16[2,2,128,128]{3,2,1,0:T(8,128)(2,1)S(1)}, u32[]{:S(2)}) copy-start(bf16[2,2,128,128]{3,2,1,0:T(8,128)(2,1)S(1)} %collective-permute-done.5.rest_3_) | copy-start | bytes 393220
where the time goes:
time: 37.2 us; the launch traced here: 37 us
  Pallas kernels  24.7 us (66%)
  starting transfers between devices  10.1 us (27%)
  local copies, waits for them, and re-layouts  1.42 us (4%)
  between operations  0.72 us (2%)
    pallas_call x1, Pallas kernels, body(): pl.pallas_call(functools.partial(prefix_kernel, scale, per_step), grid=(h...  10.4 us
    ppermute x6, starting transfers between devices, exchange(): arrived[step - 1] = lax.ppermute(sends[step - 1], 'pool', pairs)  10.1 us
    pallas_call x1, Pallas kernels, body(): pl.pallas_call(functools.partial(suffix_kernel, scale, per_step), grid=(h...  9.96 us
    pallas_call x1, Pallas kernels, body(): pl.pallas_call(fetch_kernel, out_shape=[pltpu.VMEM((fetched,) + page, dty...  2.32 us
    pallas_call x1, Pallas kernels, body(): pl.pallas_call(functools.partial(place_kernel, pages), out_shape=jax.Shap...  1.95 us
    unnamed x12, local copies, waits for them, and re-layouts  1.42 us
  transfers between devices with their start and end apart: 6, of which 0 were waited for; matrix products, arithmetic and copies ran while one was open for 0% of the time, Pallas kernels for 55%

commit v1 on v0

--- a/solution.py
+++ b/solution.py
@@ -12,6 +12,7 @@
 VMEM = pl.BlockSpec(memory_space=pltpu.VMEM)
 SMEM = pl.BlockSpec(memory_space=pltpu.SMEM)
 TILE = 256
+FIRST = 16
 
 
 def partner(index, step, groups):
@@ -84,7 +85,7 @@
 def suffix_kernel(
     scale, per_step, length_ref, start_ref, own_ref, query_ref, suffix_ref, pool_ref, *rest
 ):
-    sum_ref, top_ref, new_ref, page_ref, *back_refs, values, sem = rest
+    sum_ref, stat_ref, new_ref, key_ref, page_ref, *back_refs, values, sem = rest
     groups = len(back_refs)
     page_len, head_dim = pool_ref.shape[3:]
     suffix = query_ref.shape[0]
@@ -95,6 +96,7 @@
     @pl.when(step == 0)
     def _():
         copy.start()
+        key_ref[0] = suffix_ref[0, 0, pl.ds(0, FIRST), :]
         values[:, pl.ds(0, head_dim)] = suffix_ref[1, 0]
         values[:, pl.ds(head_dim, head_dim)] = jnp.ones((suffix, head_dim), values.dtype)
         me = lax.axis_index("pool")
@@ -112,6 +114,7 @@
     seen = lax.broadcasted_iota(jnp.int32, (tile, tile), 1) <= lax.broadcasted_iota(
         jnp.int32, (tile, tile), 0
     )
+    lane = lax.broadcasted_iota(jnp.int32, (tile, head_dim), 1)
 
     def scores_of(item):
         column, row = item
@@ -136,10 +139,9 @@
             ],
         )
         rows = pl.ds(row, tile)
-        sum_ref[rows, pl.ds(column * 2 * head_dim, 2 * head_dim)] = mixed
-        top_ref[rows, pl.ds(column * head_dim, head_dim)] = jnp.broadcast_to(
-            top, (tile, head_dim)
-        )
+        sum_ref[rows, pl.ds(column * head_dim, head_dim)] = mixed[:, :head_dim]
+        stat = jnp.where(lane == column, top, stat_ref[0, rows, :])
+        stat_ref[0, rows, :] = jnp.where(lane == per_step + column, mixed[:, head_dim:], stat)
 
     staggered(
         [(column, row) for column in range(per_step) for row in range(0, suffix, tile)],
@@ -153,7 +155,7 @@
 
 
 def prefix_kernel(
-    scale, per_step, length_ref, start_ref, query_ref, suffix_ref, sum_ref, top_ref, *rest
+    scale, per_step, length_ref, start_ref, query_ref, key_ref, sum_ref, stat_ref, *rest
 ):
     *page_refs, out_ref, keys, values = rest
     groups = len(page_refs)
@@ -181,7 +183,7 @@
                 @pl.when(jnp.logical_not(seen))
                 def _():
                     keys[rows, :] = jnp.broadcast_to(
-                        suffix_ref[0, 0, pl.ds(0, 1), :], (page_len, head_dim)
+                        key_ref[0, pl.ds(0, 1), :], (page_len, head_dim)
                     )
                     values[rows, :] = jnp.zeros((page_len, 2 * head_dim), values.dtype)
 
@@ -196,7 +198,10 @@
         column, row = item
         rows = pl.ds(row, tile)
         lanes = pl.ds(column * head_dim, head_dim)
-        before = top_ref[rows, lanes]
+        before, count = [
+            jnp.broadcast_to(stat_ref[0, rows, pl.ds(place, 1)], (tile, head_dim))
+            for place in (column, per_step + column)
+        ]
         top = jnp.maximum(before, jnp.max(score, axis=1, keepdims=True))
         factor = jnp.exp2((before - top) * scale)
         weight = jnp.concatenate(
@@ -207,10 +212,8 @@
             axis=1,
         )
         mixed = dot(weight, values[...], ALONG)
-        sums = sum_ref[rows, pl.ds(column * 2 * head_dim, head_dim)]
-        count = sum_ref[rows, pl.ds(column * 2 * head_dim + head_dim, head_dim)]
         total = mixed[:, head_dim:] + count * factor
-        out_ref[rows, lanes] = ((mixed[:, :head_dim] + sums * factor) / total).astype(
+        out_ref[rows, lanes] = ((mixed[:, :head_dim] + sum_ref[rows, lanes] * factor) / total).astype(
             out_ref.dtype
         )
 
@@ -253,10 +256,14 @@
     per_step = math.gcd(per_kv, 4)
     steps = per_kv // per_step
     scale = math.log2(math.e) / math.sqrt(head_dim)
+
+    def grant(size):
+        return pltpu.CompilerParams(vmem_limit_bytes=size * 1024 * 1024)
+
     total = fetched * groups * page_len
-    params = pltpu.CompilerParams(vmem_limit_bytes=60 * 1024 * 1024)
     columns = pl.BlockSpec((suffix, per_step * head_dim), lambda h, s: (0, h * steps + s))
-    doubled = pl.BlockSpec((suffix, 2 * per_step * head_dim), lambda h, s: (0, h * steps + s))
+    stats = pl.BlockSpec((1, suffix, head_dim), lambda h, s: (h * steps + s, 0, 0))
+    first_keys = pl.BlockSpec((1, FIRST, head_dim), lambda h, s: (h, 0, 0))
     pages_of = pl.BlockSpec((fetched, 2, 1, page_len, head_dim), lambda h, s: (0, 0, h, 0, 0))
 
     def cost(keys):
@@ -265,13 +272,14 @@
             flops=6 * cells * head_dim, bytes_accessed=8 * queries.size, transcendentals=cells
         )
 
-    sums, tops, new_pool, own_pages, own_back, *back_sends = pl.pallas_call(
+    sums, counts, new_pool, keys, own_pages, own_back, *back_sends = pl.pallas_call(
         functools.partial(suffix_kernel, scale, per_step),
         grid=(heads, steps),
         out_shape=[
-            jax.ShapeDtypeStruct((suffix, 2 * queries.shape[1]), jnp.float32),
             jax.ShapeDtypeStruct(queries.shape, jnp.float32),
+            jax.ShapeDtypeStruct((heads * steps, suffix, head_dim), jnp.float32),
             jax.ShapeDtypeStruct(pool_kv.shape, dtype),
+            jax.ShapeDtypeStruct((heads, FIRST, head_dim), dtype),
             jax.ShapeDtypeStruct((fetched,) + page, dtype),
         ]
         + [jax.ShapeDtypeStruct(page, dtype)] * groups,
@@ -283,13 +291,13 @@
             pl.BlockSpec((2, 1, suffix, head_dim), lambda h, s: (0, h, 0, 0)),
             pl.BlockSpec((2, 1, slots, page_len, head_dim), lambda h, s: (0, h, 0, 0, 0)),
         ],
-        out_specs=[doubled, columns, HBM, pages_of]
+        out_specs=[columns, stats, HBM, first_keys, pages_of]
         + [pl.BlockSpec((2, 1, page_len, head_dim), lambda h, s: (0, h, 0, 0))] * groups,
         scratch_shapes=[
             pltpu.VMEM((suffix, 2 * head_dim), dtype),
             pltpu.SemaphoreType.DMA(()),
         ],
-        compiler_params=params,
+        compiler_params=grant(60),
         cost_estimate=cost(suffix),
         name="attend_suffix",
     )(prefix_pages, owner_start, own_slots, queries, suffix_kv, pool_kv)
@@ -303,9 +311,9 @@
             SMEM,
             SMEM,
             columns,
-            pl.BlockSpec((1, 1, page_len, head_dim), lambda h, s: (0, h, 0, 0)),
-            doubled,
+            first_keys,
             columns,
+            stats,
         ]
         + [pages_of] * groups,
         out_specs=columns,
@@ -313,10 +321,10 @@
             pltpu.VMEM((total, head_dim), dtype),
             pltpu.VMEM((total, 2 * head_dim), dtype),
         ],
-        compiler_params=params,
+        compiler_params=grant(60),
         cost_estimate=cost(total),
         name="attend_prefix",
-    )(prefix_pages, owner_start, queries, suffix_kv, sums, tops, own_pages, *received)
+    )(prefix_pages, owner_start, queries, keys, sums, counts, own_pages, *received)
 
     new_pool = pl.pallas_call(
         functools.partial(place_kernel, pages),
@@ -325,7 +333,7 @@
         out_specs=HBM,
         input_output_aliases={4 + groups: 0},
         scratch_shapes=[pltpu.SemaphoreType.DMA((groups,))],
-        compiler_params=params,
+        compiler_params=grant(60),
         name="place_pages",
     )(prefix_pages, owner_start, slot_of, own_back, *returned, result, new_pool)
     return (result, new_pool)

time: 37.2 us -> 39 us (1.048)
  Pallas kernels: 24.7 us -> 26.5 us
    pallas_call x1, Pallas kernels: 10.4 us -> 13.5 us  [body(): pl.pallas_call(functools.partial(prefix_kernel, scale, per_step), grid=(h...]
    pallas_call x1, Pallas kernels: 9.96 us -> 8.72 us  [body(): pl.pallas_call(functools.partial(suffix_kernel, scale, per_step), grid=(h...]
  transfers between devices with their start and end apart: 6 -> 6, of which waited for: 0 -> 0; matrix products, arithmetic and copies ran while one was open for 0% -> 0% of each run, Pallas kernels for 55% -> 57%
where the time goes in v1:
time: 39 us; the launch traced here: 38.8 us
  Pallas kernels  26.5 us (68%)
  starting transfers between devices  10.1 us (26%)
  local copies, waits for them, and re-layouts  1.4 us (4%)
  between operations  0.73 us (2%)
    pallas_call x1, Pallas kernels, body(): pl.pallas_call(functools.partial(prefix_kernel, scale, per_step), grid=(h...  13.5 us
    ppermute x6, starting transfers between devices, exchange(): arrived[step - 1] = lax.ppermute(sends[step - 1], 'pool', pairs)  10.1 us
    pallas_call x1, Pallas kernels, body(): pl.pallas_call(functools.partial(suffix_kernel, scale, per_step), grid=(h...  8.72 us
    pallas_call x1, Pallas kernels, body(): pl.pallas_call(fetch_kernel, out_shape=[pltpu.VMEM((fetched,) + page, dty...  2.32 us
    pallas_call x1, Pallas kernels, body(): pl.pallas_call(functools.partial(place_kernel, pages), out_shape=jax.Shap...  1.95 us
    unnamed x12, local copies, waits for them, and re-layouts  1.4 us
  transfers between devices with their start and end apart: 6, of which 0 were waited for; matrix products, arithmetic and copies ran while one was open for 0% of the time, Pallas kernels for 57%

profile of v1, /device:TPU:0, one launch (start us, length us, event | category | flops | bytes accessed | tf_op | source)
XLA Modules:
  0.0 38.8 jit_solution(609707007694367199)
XLA Ops:
  0.6 2.3 %gather_pages.1 = (bf16[1,2,2,128,128]{4,3,2,1,0:T(8,128)(2,1)S(1)}, bf16[1,2,2,128,128]{4,3,2,1,0:T(8,128)(2,1)S(1)}, bf16[1,2,2,128,128]{4,3,2,1,0:T(8,128)(2,1)S(1)}, s32[1]{0:T(128)}) custom-call(s32[4,2,4]{2,1,0:T(2,128)} %bitcast.1, bf16[2,2,8,128,128]{4,3,2,1,0:T(8,128)(2,1)} %pool_ref.3), custom_call_target="tpu_custom_call" | custom-call | tf_op jit(solution)/shard_map/gather_pages/pallas_call | solution.py:245
  3.0 3.1 %collective-permute-start = (bf16[1,2,2,128,128]{4,3,2,1,0:T(8,128)(2,1)S(1)}, bf16[1,2,2,128,128]{4,3,2,1,0:T(8,128)(2,1)S(1)}, u32[]{:S(2)}, u32[]{:S(2)}) collective-permute-start(bf16[1,2,2,128,128]{4,3,2,1,0:T(8,128)(2,1)S(1)} %get-tuple-element.20), channel_id=1, source_target_pairs={{0,4},{4,0},{8,12},{12,8},{1,5},{5,1},{9,13},{13,9},{2,6},{6,2},{1... | collective-permute-start | bytes 393224 | tf_op jit(solution)/shard_map/ppermute | solution.py:242
  6.0 2.6 %collective-permute-start.1 = (bf16[1,2,2,128,128]{4,3,2,1,0:T(8,128)(2,1)S(1)}, bf16[1,2,2,128,128]{4,3,2,1,0:T(8,128)(2,1)S(1)}, u32[]{:S(2)}, u32[]{:S(2)}) collective-permute-start(bf16[1,2,2,128,128]{4,3,2,1,0:T(8,128)(2,1)S(1)} %get-tuple-element.21), channel_id=1, source_target_pairs={{0,8},{4,12},{8,0},{12,4},{1,9},{5,13},{9,1},{13,5},{2,10},{6,14},... | collective-permute-start | bytes 393224 | tf_op jit(solution)/shard_map/ppermute | solution.py:242
  8.6 0.0 collective-permute-start.2
  8.6 8.7 %attend_suffix.1 = (f32[512,2048]{1,0:T(8,128)}, f32[4,512,128]{2,1,0:T(8,128)}, bf16[2,2,8,128,128]{4,3,2,1,0:T(8,128)(2,1)}, bf16[2,16,128]{2,1,0:T(8,128)(2,1...) custom-call(s32[4]{0:T(128)} %length_ref.5, ...), custom_call_target="tpu_custom_call" | custom-call | flops 3221225472 | bytes 8388608 | tf_op jit(solution)/shard_map/attend_suffix/pallas_call | solution.py:275
  17.4 1.0 %collective-permute-start.3 = (bf16[2,2,128,128]{3,2,1,0:T(8,128)(2,1)}, bf16[2,2,128,128]{3,2,1,0:T(8,128)(2,1)S(1)}, u32[]{:S(2)}, u32[]{:S(2)}) collective-permute-start(bf16[2,2,128,128]{3,2,1,0:T(8,128)(2,1)} %get-tuple-element.24), channel_id=1, source_target_pairs={{0,4},{4,0},{8,12},{12,8},{1,5},{5,1},{9,13},{13,9},{2,6},{6,2},{1... | collective-permute-start | bytes 393224 | tf_op jit(solution)/shard_map/ppermute | solution.py:242
  18.3 3.5 %collective-permute-start.4 = (bf16[2,2,128,128]{3,2,1,0:T(8,128)(2,1)}, bf16[2,2,128,128]{3,2,1,0:T(8,128)(2,1)S(1)}, u32[]{:S(2)}, u32[]{:S(2)}) collective-permute-start(bf16[2,2,128,128]{3,2,1,0:T(8,128)(2,1)} %get-tuple-element.25), channel_id=1, source_target_pairs={{0,8},{4,12},{8,0},{12,4},{1,9},{5,13},{9,1},{13,5},{2,10},{6,14},... | collective-permute-start | bytes 393224 | tf_op jit(solution)/shard_map/ppermute | solution.py:242
  21.8 0.0 collective-permute-done.rest_1_
  21.8 0.0 copy-start.3
  21.8 0.0 collective-permute-start.5
  21.8 0.0 collective-permute-done.1.rest_2_
  21.8 0.0 copy-start.4
  21.9 0.0 collective-permute-done.2.rest_3_
  21.9 0.0 copy-start.5
  21.9 0.6 %copy-done.3 = bf16[1,2,2,128,128]{4,3,2,1,0:T(8,128)(2,1)} copy-done((bf16[1,2,2,128,128]{4,3,2,1,0:T(8,128)(2,1)}, bf16[1,2,2,128,128]{4,3,2,1,0:T(8,128)(2,1)S(1)}, u32[]{:S(2)}) %copy-start.3) | copy-done | bytes 131096
  22.5 0.0 copy-done.4
  22.5 0.1 copy-done.5
  22.6 13.5 %attend_prefix.1.rest_4_ = bf16[512,2048]{1,0:T(8,128)(2,1)} custom-call(s32[4]{0:T(128)} %length_ref.5, s32[4]{0:T(128)} %start_ref.5, bf16[512,2048]{1,0:T(8,128)(2,1)} %query_ref.3, bf16[2,16,128]{2,1,0:T(8,128)(2,1)} %get-tuple-element.16.key_ref, f32[512,2048]{1,0:T(8,128)} %get-tuple-element.17.sum_ref, f32[4,512,128]{2,1,0:T(8,128)} %get-tuple-element.18.stat_ref, ...), custom_call_target="tpu_custom_call" | custom-call | flops 3221225472 | bytes 8388608 | tf_op jit(solution)/shard_map/attend_prefix/pallas_call | solution.py:306
  36.0 0.0 collective-permute-done.3.rest_1_
  36.1 0.0 copy-start
  36.1 0.0 collective-permute-done.4.rest_2_
  36.1 0.0 copy-start.1
  36.1 0.0 collective-permute-done.5.rest_3_
  36.1 0.0 copy-start.2
  36.1 0.6 %copy-done = bf16[2,2,128,128]{3,2,1,0:T(8,128)(2,1)} copy-done((bf16[2,2,128,128]{3,2,1,0:T(8,128)(2,1)}, bf16[2,2,128,128]{3,2,1,0:T(8,128)(2,1)S(1)}, u32[]{:S(2)}) %copy-start) | copy-done | bytes 131096
  36.7 0.0 copy-done.1
  36.8 0.0 copy-done.2
  36.8 2.0 %place_pages.1 = bf16[2,2,8,128,128]{4,3,2,1,0:T(8,128)(2,1)} custom-call(s32[4]{0:T(128)} %length_ref.5, s32[4]{0:T(128)} %start_ref.5, s32[4,2,4]{2,1,0:T(2,128)} %bitcast.2, bf16[2,2,128,128]{3,2,1,0:T(8,128)(2,1)} %get-tuple-element.23.rest_0_, bf16[2,2,128,128]{3,2,1,0:T(8,128)(2,1)} %copy-done, ...), custom_call_target="tpu_custom_call", output_to_operand_aliasing={{}: (8, {})} | custom-call | tf_op jit(solution)/shard_map/place_pages/pallas_call | solution.py:329
Async XLA Ops:
  3.0 18.9 %collective-permute-start = (bf16[1,2,2,128,128]{4,3,2,1,0:T(8,128)(2,1)S(1)}, bf16[1,2,2,128,128]{4,3,2,1,0:T(8,128)(2,1)S(1)}, u32[]{:S(2)}, u32[]{:S(2)}) collective-permute-start(bf16[1,2,2,128,128]{4,3,2,1,0:T(8,128)(2,1)S(1)} %get-tuple-element.20), channel_id=1, source_target_pairs={{0,4},{4,0},{8,12},{12,8},{1,5},{5,1},{9,13},{13,9},{2,6},{6,2},{1... | collective-permute-start | bytes 393224 | tf_op jit(solution)/shard_map/ppermute | solution.py:242
  6.0 15.8 %collective-permute-start.1 = (bf16[1,2,2,128,128]{4,3,2,1,0:T(8,128)(2,1)S(1)}, bf16[1,2,2,128,128]{4,3,2,1,0:T(8,128)(2,1)S(1)}, u32[]{:S(2)}, u32[]{:S(2)}) collective-permute-start(bf16[1,2,2,128,128]{4,3,2,1,0:T(8,128)(2,1)S(1)} %get-tuple-element.21), channel_id=1, source_target_pairs={{0,8},{4,12},{8,0},{12,4},{1,9},{5,13},{9,1},{13,5},{2,10},{6,14},... | collective-permute-start | bytes 393224 | tf_op jit(solution)/shard_map/ppermute | solution.py:242
  8.6 13.2 %collective-permute-start.2 = (bf16[1,2,2,128,128]{4,3,2,1,0:T(8,128)(2,1)S(1)}, bf16[1,2,2,128,128]{4,3,2,1,0:T(8,128)(2,1)S(1)}, u32[]{:S(2)}, u32[]{:S(2)}) collective-permute-start(bf16[1,2,2,128,128]{4,3,2,1,0:T(8,128)(2,1)S(1)} %get-tuple-element.22), channel_id=1, source_target_pairs={{0,12},{4,8},{8,4},{12,0},{1,13},{5,9},{9,5},{13,1},{2,14},{6,10},... | collective-permute-start | bytes 393224 | tf_op jit(solution)/shard_map/ppermute | solution.py:242
  17.4 18.7 %collective-permute-start.3 = (bf16[2,2,128,128]{3,2,1,0:T(8,128)(2,1)}, bf16[2,2,128,128]{3,2,1,0:T(8,128)(2,1)S(1)}, u32[]{:S(2)}, u32[]{:S(2)}) collective-permute-start(bf16[2,2,128,128]{3,2,1,0:T(8,128)(2,1)} %get-tuple-element.24), channel_id=1, source_target_pairs={{0,4},{4,0},{8,12},{12,8},{1,5},{5,1},{9,13},{13,9},{2,6},{6,2},{1... | collective-permute-start | bytes 393224 | tf_op jit(solution)/shard_map/ppermute | solution.py:242
  18.3 17.7 %collective-permute-start.4 = (bf16[2,2,128,128]{3,2,1,0:T(8,128)(2,1)}, bf16[2,2,128,128]{3,2,1,0:T(8,128)(2,1)S(1)}, u32[]{:S(2)}, u32[]{:S(2)}) collective-permute-start(bf16[2,2,128,128]{3,2,1,0:T(8,128)(2,1)} %get-tuple-element.25), channel_id=1, source_target_pairs={{0,8},{4,12},{8,0},{12,4},{1,9},{5,13},{9,1},{13,5},{2,10},{6,14},... | collective-permute-start | bytes 393224 | tf_op jit(solution)/shard_map/ppermute | solution.py:242
  21.8 0.7 %copy-start.3 = (bf16[1,2,2,128,128]{4,3,2,1,0:T(8,128)(2,1)}, bf16[1,2,2,128,128]{4,3,2,1,0:T(8,128)(2,1)S(1)}, u32[]{:S(2)}) copy-start(bf16[1,2,2,128,128]{4,3,2,1,0:T(8,128)(2,1)S(1)} %collective-permute-done.rest_1_) | copy-start | bytes 393220
  21.8 14.3 %collective-permute-start.5 = (bf16[2,2,128,128]{3,2,1,0:T(8,128)(2,1)}, bf16[2,2,128,128]{3,2,1,0:T(8,128)(2,1)S(1)}, u32[]{:S(2)}, u32[]{:S(2)}) collective-permute-start(bf16[2,2,128,128]{3,2,1,0:T(8,128)(2,1)} %get-tuple-element.26), channel_id=1, source_target_pairs={{0,12},{4,8},{8,4},{12,0},{1,13},{5,9},{9,5},{13,1},{2,14},{6,10},... | collective-permute-start | bytes 393224 | tf_op jit(solution)/shard_map/ppermute | solution.py:242
  21.8 0.7 %copy-start.4 = (bf16[1,2,2,128,128]{4,3,2,1,0:T(8,128)(2,1)}, bf16[1,2,2,128,128]{4,3,2,1,0:T(8,128)(2,1)S(1)}, u32[]{:S(2)}) copy-start(bf16[1,2,2,128,128]{4,3,2,1,0:T(8,128)(2,1)S(1)} %collective-permute-done.1.rest_2_) | copy-start | bytes 393220
  21.9 0.7 %copy-start.5 = (bf16[1,2,2,128,128]{4,3,2,1,0:T(8,128)(2,1)}, bf16[1,2,2,128,128]{4,3,2,1,0:T(8,128)(2,1)S(1)}, u32[]{:S(2)}) copy-start(bf16[1,2,2,128,128]{4,3,2,1,0:T(8,128)(2,1)S(1)} %collective-permute-done.2.rest_3_) | copy-start | bytes 393220
  36.1 0.7 %copy-start = (bf16[2,2,128,128]{3,2,1,0:T(8,128)(2,1)}, bf16[2,2,128,128]{3,2,1,0:T(8,128)(2,1)S(1)}, u32[]{:S(2)}) copy-start(bf16[2,2,128,128]{3,2,1,0:T(8,128)(2,1)S(1)} %collective-permute-done.3.rest_1_) | copy-start | bytes 393220
  36.1 0.7 %copy-start.1 = (bf16[2,2,128,128]{3,2,1,0:T(8,128)(2,1)}, bf16[2,2,128,128]{3,2,1,0:T(8,128)(2,1)S(1)}, u32[]{:S(2)}) copy-start(bf16[2,2,128,128]{3,2,1,0:T(8,128)(2,1)S(1)} %collective-permute-done.4.rest_2_) | copy-start | bytes 393220
  36.1 0.7 %copy-start.2 = (bf16[2,2,128,128]{3,2,1,0:T(8,128)(2,1)}, bf16[2,2,128,128]{3,2,1,0:T(8,128)(2,1)S(1)}, u32[]{:S(2)}) copy-start(bf16[2,2,128,128]{3,2,1,0:T(8,128)(2,1)S(1)} %collective-permute-done.5.rest_3_) | copy-start | bytes 393220

commit v2 on v1

--- a/solution.py
+++ b/solution.py
@@ -85,7 +85,7 @@
 def suffix_kernel(
     scale, per_step, length_ref, start_ref, own_ref, query_ref, suffix_ref, pool_ref, *rest
 ):
-    sum_ref, stat_ref, new_ref, key_ref, page_ref, *back_refs, values, sem = rest
+    mean_ref, log_ref, new_ref, key_ref, page_ref, *back_refs, values, sem = rest
     groups = len(back_refs)
     page_len, head_dim = pool_ref.shape[3:]
     suffix = query_ref.shape[0]
@@ -114,40 +114,52 @@
     seen = lax.broadcasted_iota(jnp.int32, (tile, tile), 1) <= lax.broadcasted_iota(
         jnp.int32, (tile, tile), 0
     )
-    lane = lax.broadcasted_iota(jnp.int32, (tile, head_dim), 1)
-
-    def scores_of(item):
-        column, row = item
-        query = query_ref[pl.ds(row, tile), pl.ds(column * head_dim, head_dim)]
-        score = dot(query, suffix_ref[0, 0, pl.ds(row, tile), :], ACROSS)
-        parts = [(jnp.where(seen, score, -jnp.inf), pl.ds(row, tile))]
-        if row:
-            early = pl.ds(0, row)
-            parts.append((dot(query, suffix_ref[0, 0, early, :], ACROSS), early))
-        return parts
-
-    def finish(item, parts):
-        column, row = item
-        top = functools.reduce(
-            jnp.maximum, [jnp.max(score, axis=1, keepdims=True) for score, _ in parts]
-        )
-        mixed = functools.reduce(
-            jnp.add,
+
+    def scores_of(column):
+        lanes = pl.ds(column * head_dim, head_dim)
+        return [
+            dot(query_ref[row:, lanes], suffix_ref[0, 0, pl.ds(row, tile), :], ACROSS)
+            for row in range(0, suffix, tile)
+        ]
+
+    def finish(column, scores):
+        lanes = pl.ds(column * head_dim, head_dim)
+        scores = [
             [
-                dot(jnp.exp2((score - top) * scale).astype(jnp.bfloat16), values[keys, :], ALONG)
-                for score, keys in parts
-            ],
-        )
-        rows = pl.ds(row, tile)
-        sum_ref[rows, pl.ds(column * head_dim, head_dim)] = mixed[:, :head_dim]
-        stat = jnp.where(lane == column, top, stat_ref[0, rows, :])
-        stat_ref[0, rows, :] = jnp.where(lane == per_step + column, mixed[:, head_dim:], stat)
-
-    staggered(
-        [(column, row) for column in range(per_step) for row in range(0, suffix, tile)],
-        scores_of,
-        finish,
-    )
+                block[row : row + tile] if row else jnp.where(seen, block[:tile], -jnp.inf)
+                for row in range(0, block.shape[0], tile)
+            ]
+            for block in scores
+        ]
+        blocks = len(scores)
+        tops = [
+            functools.reduce(
+                jnp.maximum,
+                [
+                    jnp.max(scores[key][row - key], axis=1, keepdims=True)
+                    for key in range(row + 1)
+                ],
+            )
+            for row in range(blocks)
+        ]
+        mixed = [None] * blocks
+        for key in range(blocks):
+            weight = [
+                jnp.exp2((scores[key][row - key] - tops[row]) * scale).astype(jnp.bfloat16)
+                for row in range(key, blocks)
+            ]
+            weight = jnp.concatenate(weight, axis=0) if len(weight) > 1 else weight[0]
+            part = dot(weight, values[pl.ds(key * tile, tile), :], ALONG)
+            for row in range(key, blocks):
+                piece = part[(row - key) * tile : (row - key + 1) * tile]
+                mixed[row] = piece if mixed[row] is None else mixed[row] + piece
+        for row in range(blocks):
+            rows = pl.ds(row * tile, tile)
+            count = mixed[row][:, head_dim:]
+            mean_ref[rows, lanes] = mixed[row][:, :head_dim] / count
+            log_ref[rows, lanes] = tops[row] * scale + jnp.log2(count)
+
+    staggered(range(per_step), scores_of, finish)
 
     @pl.when(step == pl.num_programs(1) - 1)
     def _():
@@ -155,7 +167,7 @@
 
 
 def prefix_kernel(
-    scale, per_step, length_ref, start_ref, query_ref, key_ref, sum_ref, stat_ref, *rest
+    scale, per_step, length_ref, start_ref, query_ref, key_ref, mean_ref, log_ref, *rest
 ):
     *page_refs, out_ref, keys, values = rest
     groups = len(page_refs)
@@ -187,41 +199,28 @@
                     )
                     values[rows, :] = jnp.zeros((page_len, 2 * head_dim), values.dtype)
 
-    tile = min(TILE, suffix)
-
-    def scores_of(item):
-        column, row = item
-        query = query_ref[pl.ds(row, tile), pl.ds(column * head_dim, head_dim)]
+    def scores_of(column):
+        query = query_ref[:, pl.ds(column * head_dim, head_dim)]
         return dot(query, keys[...], ACROSS)
 
-    def finish(item, score):
-        column, row = item
-        rows = pl.ds(row, tile)
+    def finish(column, score):
         lanes = pl.ds(column * head_dim, head_dim)
-        before, count = [
-            jnp.broadcast_to(stat_ref[0, rows, pl.ds(place, 1)], (tile, head_dim))
-            for place in (column, per_step + column)
-        ]
-        top = jnp.maximum(before, jnp.max(score, axis=1, keepdims=True))
-        factor = jnp.exp2((before - top) * scale)
+        before = log_ref[:, lanes]
+        top = jnp.maximum(before, jnp.max(score, axis=1, keepdims=True) * scale)
         weight = jnp.concatenate(
             [
-                jnp.exp2((score[:, start : start + head_dim] - top) * scale).astype(jnp.bfloat16)
+                jnp.exp2(score[:, start : start + head_dim] * scale - top).astype(jnp.bfloat16)
                 for start in range(0, score.shape[1], head_dim)
             ],
             axis=1,
         )
         mixed = dot(weight, values[...], ALONG)
-        total = mixed[:, head_dim:] + count * factor
-        out_ref[rows, lanes] = ((mixed[:, :head_dim] + sum_ref[rows, lanes] * factor) / total).astype(
-            out_ref.dtype
-        )
-
-    staggered(
-        [(column, row) for column in range(per_step) for row in range(0, suffix, tile)],
-        scores_of,
-        finish,
-    )
+        share = jnp.exp2(before - top)
+        out_ref[:, lanes] = (
+            (mixed[:, :head_dim] + mean_ref[:, lanes] * share) / (mixed[:, head_dim:] + share)
+        ).astype(out_ref.dtype)
+
+    staggered(range(per_step), scores_of, finish)
 
 
 def body(queries, suffix_kv, pool_kv, prefix_pages, owner_start, page_slot):
@@ -262,7 +261,6 @@
 
     total = fetched * groups * page_len
     columns = pl.BlockSpec((suffix, per_step * head_dim), lambda h, s: (0, h * steps + s))
-    stats = pl.BlockSpec((1, suffix, head_dim), lambda h, s: (h * steps + s, 0, 0))
     first_keys = pl.BlockSpec((1, FIRST, head_dim), lambda h, s: (h, 0, 0))
     pages_of = pl.BlockSpec((fetched, 2, 1, page_len, head_dim), lambda h, s: (0, 0, h, 0, 0))
 
@@ -272,12 +270,12 @@
             flops=6 * cells * head_dim, bytes_accessed=8 * queries.size, transcendentals=cells
         )
 
-    sums, counts, new_pool, keys, own_pages, own_back, *back_sends = pl.pallas_call(
+    means, logs, new_pool, keys, own_pages, own_back, *back_sends = pl.pallas_call(
         functools.partial(suffix_kernel, scale, per_step),
         grid=(heads, steps),
         out_shape=[
             jax.ShapeDtypeStruct(queries.shape, jnp.float32),
-            jax.ShapeDtypeStruct((heads * steps, suffix, head_dim), jnp.float32),
+            jax.ShapeDtypeStruct(queries.shape, jnp.float32),
             jax.ShapeDtypeStruct(pool_kv.shape, dtype),
             jax.ShapeDtypeStruct((heads, FIRST, head_dim), dtype),
             jax.ShapeDtypeStruct((fetched,) + page, dtype),
@@ -291,7 +289,7 @@
             pl.BlockSpec((2, 1, suffix, head_dim), lambda h, s: (0, h, 0, 0)),
             pl.BlockSpec((2, 1, slots, page_len, head_dim), lambda h, s: (0, h, 0, 0, 0)),
         ],
-        out_specs=[columns, stats, HBM, first_keys, pages_of]
+        out_specs=[columns, columns, HBM, first_keys, pages_of]
         + [pl.BlockSpec((2, 1, page_len, head_dim), lambda h, s: (0, h, 0, 0))] * groups,
         scratch_shapes=[
             pltpu.VMEM((suffix, 2 * head_dim), dtype),
@@ -313,7 +311,7 @@
             columns,
             first_keys,
             columns,
-            stats,
+            columns,
         ]
         + [pages_of] * groups,
         out_specs=columns,
@@ -324,7 +322,7 @@
         compiler_params=grant(60),
         cost_estimate=cost(total),
         name="attend_prefix",
-    )(prefix_pages, owner_start, queries, keys, sums, counts, own_pages, *received)
+    )(prefix_pages, owner_start, queries, keys, means, logs, own_pages, *received)
 
     new_pool = pl.pallas_call(
         functools.partial(place_kernel, pages),

time: 39 us -> 36.1 us (0.926)
  Pallas kernels: 26.5 us -> 23.4 us
    pallas_call x1, Pallas kernels: 13.5 us -> 9.57 us  [body(): pl.pallas_call(functools.partial(prefix_kernel, scale, per_step), grid=(h...]
    pallas_call x1, Pallas kernels: 8.72 us -> 9.54 us  [body(): pl.pallas_call(functools.partial(suffix_kernel, scale, per_step), grid=(h...]
  transfers between devices with their start and end apart: 6 -> 6, of which waited for: 0 -> 0; matrix products, arithmetic and copies ran while one was open for 0% -> 0% of each run, Pallas kernels for 57% -> 54%
where the time goes in v2:
time: 36.1 us; the launch traced here: 35.7 us
  Pallas kernels  23.4 us (65%)
  starting transfers between devices  10.1 us (28%)
  local copies, waits for them, and re-layouts  1.44 us (4%)
  between operations  0.72 us (2%)
    ppermute x6, starting transfers between devices, exchange(): arrived[step - 1] = lax.ppermute(sends[step - 1], 'pool', pairs)  10.1 us
    pallas_call x1, Pallas kernels, body(): pl.pallas_call(functools.partial(prefix_kernel, scale, per_step), grid=(h...  9.57 us
    pallas_call x1, Pallas kernels, body(): pl.pallas_call(functools.partial(suffix_kernel, scale, per_step), grid=(h...  9.54 us
    pallas_call x1, Pallas kernels, body(): pl.pallas_call(fetch_kernel, out_shape=[pltpu.VMEM((fetched,) + page, dty...  2.32 us
    pallas_call x1, Pallas kernels, body(): pl.pallas_call(functools.partial(place_kernel, pages), out_shape=jax.Shap...  1.95 us
    unnamed x12, local copies, waits for them, and re-layouts  1.44 us
  transfers between devices with their start and end apart: 6, of which 0 were waited for; matrix products, arithmetic and copies ran while one was open for 0% of the time, Pallas kernels for 54%

profile of v2, /device:TPU:0, one launch (start us, length us, event | category | flops | bytes accessed | tf_op | source)
XLA Modules:
  0.0 35.7 jit_solution(4058939529455672996)
XLA Ops:
  0.6 2.3 %gather_pages.1 = (bf16[1,2,2,128,128]{4,3,2,1,0:T(8,128)(2,1)S(1)}, bf16[1,2,2,128,128]{4,3,2,1,0:T(8,128)(2,1)S(1)}, bf16[1,2,2,128,128]{4,3,2,1,0:T(8,128)(2,1)S(1)}, s32[1]{0:T(128)}) custom-call(s32[4,2,4]{2,1,0:T(2,128)} %bitcast.1, bf16[2,2,8,128,128]{4,3,2,1,0:T(8,128)(2,1)} %pool_ref.3), custom_call_target="tpu_custom_call" | custom-call | tf_op jit(solution)/shard_map/gather_pages/pallas_call | solution.py:244
  3.0 3.1 %collective-permute-start = (bf16[1,2,2,128,128]{4,3,2,1,0:T(8,128)(2,1)S(1)}, bf16[1,2,2,128,128]{4,3,2,1,0:T(8,128)(2,1)S(1)}, u32[]{:S(2)}, u32[]{:S(2)}) collective-permute-start(bf16[1,2,2,128,128]{4,3,2,1,0:T(8,128)(2,1)S(1)} %get-tuple-element.20), channel_id=1, source_target_pairs={{0,4},{4,0},{8,12},{12,8},{1,5},{5,1},{9,13},{13,9},{2,6},{6,2},{1... | collective-permute-start | bytes 393224 | tf_op jit(solution)/shard_map/ppermute | solution.py:241
  6.0 2.6 %collective-permute-start.1 = (bf16[1,2,2,128,128]{4,3,2,1,0:T(8,128)(2,1)S(1)}, bf16[1,2,2,128,128]{4,3,2,1,0:T(8,128)(2,1)S(1)}, u32[]{:S(2)}, u32[]{:S(2)}) collective-permute-start(bf16[1,2,2,128,128]{4,3,2,1,0:T(8,128)(2,1)S(1)} %get-tuple-element.21), channel_id=1, source_target_pairs={{0,8},{4,12},{8,0},{12,4},{1,9},{5,13},{9,1},{13,5},{2,10},{6,14},... | collective-permute-start | bytes 393224 | tf_op jit(solution)/shard_map/ppermute | solution.py:241
  8.6 0.0 collective-permute-start.2
  8.6 9.5 %attend_suffix.1 = (f32[512,2048]{1,0:T(8,128)}, f32[512,2048]{1,0:T(8,128)}, bf16[2,2,8,128,128]{4,3,2,1,0:T(8,128)(2,1)}, bf16[2,16,128]{2,1,0:T(8,128)(2,1)},...) custom-call(s32[4]{0:T(128)} %length_ref.5, ...), custom_call_target="tpu_custom_call" | custom-call | flops 3221225472 | bytes 8388608 | tf_op jit(solution)/shard_map/attend_suffix/pallas_call | solution.py:273
  18.2 1.0 %collective-permute-start.3 = (bf16[2,2,128,128]{3,2,1,0:T(8,128)(2,1)}, bf16[2,2,128,128]{3,2,1,0:T(8,128)(2,1)S(1)}, u32[]{:S(2)}, u32[]{:S(2)}) collective-permute-start(bf16[2,2,128,128]{3,2,1,0:T(8,128)(2,1)} %get-tuple-element.24), channel_id=1, source_target_pairs={{0,4},{4,0},{8,12},{12,8},{1,5},{5,1},{9,13},{13,9},{2,6},{6,2},{1... | collective-permute-start | bytes 393224 | tf_op jit(solution)/shard_map/ppermute | solution.py:241
  19.1 3.5 %collective-permute-start.4 = (bf16[2,2,128,128]{3,2,1,0:T(8,128)(2,1)}, bf16[2,2,128,128]{3,2,1,0:T(8,128)(2,1)S(1)}, u32[]{:S(2)}, u32[]{:S(2)}) collective-permute-start(bf16[2,2,128,128]{3,2,1,0:T(8,128)(2,1)} %get-tuple-element.25), channel_id=1, source_target_pairs={{0,8},{4,12},{8,0},{12,4},{1,9},{5,13},{9,1},{13,5},{2,10},{6,14},... | collective-permute-start | bytes 393224 | tf_op jit(solution)/shard_map/ppermute | solution.py:241
  22.6 0.0 collective-permute-done.rest_1_
  22.6 0.0 copy-start
  22.6 0.0 collective-permute-start.5
  22.7 0.0 collective-permute-done.1.rest_2_
  22.7 0.0 copy-start.1
  22.7 0.0 collective-permute-done.2.rest_3_
  22.7 0.0 copy-start.2
  22.7 0.6 %copy-done = bf16[1,2,2,128,128]{4,3,2,1,0:T(8,128)(2,1)} copy-done((bf16[1,2,2,128,128]{4,3,2,1,0:T(8,128)(2,1)}, bf16[1,2,2,128,128]{4,3,2,1,0:T(8,128)(2,1)S(1)}, u32[]{:S(2)}) %copy-start) | copy-done | bytes 131096
  23.3 0.1 copy-done.1
  23.4 0.1 copy-done.2
  23.4 9.6 %attend_prefix.1.rest_4_ = bf16[512,2048]{1,0:T(8,128)(2,1)} custom-call(s32[4]{0:T(128)} %length_ref.5, s32[4]{0:T(128)} %start_ref.5, bf16[512,2048]{1,0:T(8,128)(2,1)} %query_ref.3, bf16[2,16,128]{2,1,0:T(8,128)(2,1)} %get-tuple-element.16.key_ref, f32[512,2048]{1,0:T(8,128)} %get-tuple-element.17.mean_ref, f32[512,2048]{1,0:T(8,128)} %get-tuple-element.18.log_ref, ...), custom_call_target="tpu_custom_call" | custom-call | flops 3221225472 | bytes 8388608 | tf_op jit(solution)/shard_map/attend_prefix/pallas_call | solution.py:304
  33.0 0.0 collective-permute-done.3.rest_1_
  33.0 0.0 copy-start.3
  33.0 0.0 collective-permute-done.4.rest_2_
  33.0 0.0 copy-start.4
  33.0 0.0 collective-permute-done.5.rest_3_
  33.0 0.0 copy-start.5
  33.1 0.6 %copy-done.3 = bf16[2,2,128,128]{3,2,1,0:T(8,128)(2,1)} copy-done((bf16[2,2,128,128]{3,2,1,0:T(8,128)(2,1)}, bf16[2,2,128,128]{3,2,1,0:T(8,128)(2,1)S(1)}, u32[]{:S(2)}) %copy-start.3) | copy-done | bytes 131096
  33.7 0.0 copy-done.4
  33.7 0.0 copy-done.5
  33.7 2.0 %place_pages.1 = bf16[2,2,8,128,128]{4,3,2,1,0:T(8,128)(2,1)} custom-call(s32[4]{0:T(128)} %length_ref.5, s32[4]{0:T(128)} %start_ref.5, s32[4,2,4]{2,1,0:T(2,128)} %bitcast.2, bf16[2,2,128,128]{3,2,1,0:T(8,128)(2,1)} %get-tuple-element.23.rest_0_, bf16[2,2,128,128]{3,2,1,0:T(8,128)(2,1)} %copy-done.3, ...), custom_call_target="tpu_custom_call", output_to_operand_aliasing={{}: (8, {})} | custom-call | tf_op jit(solution)/shard_map/place_pages/pallas_call | solution.py:327
Async XLA Ops:
  3.0 19.7 %collective-permute-start = (bf16[1,2,2,128,128]{4,3,2,1,0:T(8,128)(2,1)S(1)}, bf16[1,2,2,128,128]{4,3,2,1,0:T(8,128)(2,1)S(1)}, u32[]{:S(2)}, u32[]{:S(2)}) collective-permute-start(bf16[1,2,2,128,128]{4,3,2,1,0:T(8,128)(2,1)S(1)} %get-tuple-element.20), channel_id=1, source_target_pairs={{0,4},{4,0},{8,12},{12,8},{1,5},{5,1},{9,13},{13,9},{2,6},{6,2},{1... | collective-permute-start | bytes 393224 | tf_op jit(solution)/shard_map/ppermute | solution.py:241
  6.0 16.6 %collective-permute-start.1 = (bf16[1,2,2,128,128]{4,3,2,1,0:T(8,128)(2,1)S(1)}, bf16[1,2,2,128,128]{4,3,2,1,0:T(8,128)(2,1)S(1)}, u32[]{:S(2)}, u32[]{:S(2)}) collective-permute-start(bf16[1,2,2,128,128]{4,3,2,1,0:T(8,128)(2,1)S(1)} %get-tuple-element.21), channel_id=1, source_target_pairs={{0,8},{4,12},{8,0},{12,4},{1,9},{5,13},{9,1},{13,5},{2,10},{6,14},... | collective-permute-start | bytes 393224 | tf_op jit(solution)/shard_map/ppermute | solution.py:241
  8.6 14.0 %collective-permute-start.2 = (bf16[1,2,2,128,128]{4,3,2,1,0:T(8,128)(2,1)S(1)}, bf16[1,2,2,128,128]{4,3,2,1,0:T(8,128)(2,1)S(1)}, u32[]{:S(2)}, u32[]{:S(2)}) collective-permute-start(bf16[1,2,2,128,128]{4,3,2,1,0:T(8,128)(2,1)S(1)} %get-tuple-element.22), channel_id=1, source_target_pairs={{0,12},{4,8},{8,4},{12,0},{1,13},{5,9},{9,5},{13,1},{2,14},{6,10},... | collective-permute-start | bytes 393224 | tf_op jit(solution)/shard_map/ppermute | solution.py:241
  18.2 14.8 %collective-permute-start.3 = (bf16[2,2,128,128]{3,2,1,0:T(8,128)(2,1)}, bf16[2,2,128,128]{3,2,1,0:T(8,128)(2,1)S(1)}, u32[]{:S(2)}, u32[]{:S(2)}) collective-permute-start(bf16[2,2,128,128]{3,2,1,0:T(8,128)(2,1)} %get-tuple-element.24), channel_id=1, source_target_pairs={{0,4},{4,0},{8,12},{12,8},{1,5},{5,1},{9,13},{13,9},{2,6},{6,2},{1... | collective-permute-start | bytes 393224 | tf_op jit(solution)/shard_map/ppermute | solution.py:241
  19.1 13.9 %collective-permute-start.4 = (bf16[2,2,128,128]{3,2,1,0:T(8,128)(2,1)}, bf16[2,2,128,128]{3,2,1,0:T(8,128)(2,1)S(1)}, u32[]{:S(2)}, u32[]{:S(2)}) collective-permute-start(bf16[2,2,128,128]{3,2,1,0:T(8,128)(2,1)} %get-tuple-element.25), channel_id=1, source_target_pairs={{0,8},{4,12},{8,0},{12,4},{1,9},{5,13},{9,1},{13,5},{2,10},{6,14},... | collective-permute-start | bytes 393224 | tf_op jit(solution)/shard_map/ppermute | solution.py:241
  22.6 0.7 %copy-start = (bf16[1,2,2,128,128]{4,3,2,1,0:T(8,128)(2,1)}, bf16[1,2,2,128,128]{4,3,2,1,0:T(8,128)(2,1)S(1)}, u32[]{:S(2)}) copy-start(bf16[1,2,2,128,128]{4,3,2,1,0:T(8,128)(2,1)S(1)} %collective-permute-done.rest_1_) | copy-start | bytes 393220
  22.6 10.4 %collective-permute-start.5 = (bf16[2,2,128,128]{3,2,1,0:T(8,128)(2,1)}, bf16[2,2,128,128]{3,2,1,0:T(8,128)(2,1)S(1)}, u32[]{:S(2)}, u32[]{:S(2)}) collective-permute-start(bf16[2,2,128,128]{3,2,1,0:T(8,128)(2,1)} %get-tuple-element.26), channel_id=1, source_target_pairs={{0,12},{4,8},{8,4},{12,0},{1,13},{5,9},{9,5},{13,1},{2,14},{6,10},... | collective-permute-start | bytes 393224 | tf_op jit(solution)/shard_map/ppermute | solution.py:241
  22.7 0.7 %copy-start.1 = (bf16[1,2,2,128,128]{4,3,2,1,0:T(8,128)(2,1)}, bf16[1,2,2,128,128]{4,3,2,1,0:T(8,128)(2,1)S(1)}, u32[]{:S(2)}) copy-start(bf16[1,2,2,128,128]{4,3,2,1,0:T(8,128)(2,1)S(1)} %collective-permute-done.1.rest_2_) | copy-start | bytes 393220
  22.7 0.7 %copy-start.2 = (bf16[1,2,2,128,128]{4,3,2,1,0:T(8,128)(2,1)}, bf16[1,2,2,128,128]{4,3,2,1,0:T(8,128)(2,1)S(1)}, u32[]{:S(2)}) copy-start(bf16[1,2,2,128,128]{4,3,2,1,0:T(8,128)(2,1)S(1)} %collective-permute-done.2.rest_3_) | copy-start | bytes 393220
  33.0 0.7 %copy-start.3 = (bf16[2,2,128,128]{3,2,1,0:T(8,128)(2,1)}, bf16[2,2,128,128]{3,2,1,0:T(8,128)(2,1)S(1)}, u32[]{:S(2)}) copy-start(bf16[2,2,128,128]{3,2,1,0:T(8,128)(2,1)S(1)} %collective-permute-done.3.rest_1_) | copy-start | bytes 393220
  33.0 0.7 %copy-start.4 = (bf16[2,2,128,128]{3,2,1,0:T(8,128)(2,1)}, bf16[2,2,128,128]{3,2,1,0:T(8,128)(2,1)S(1)}, u32[]{:S(2)}) copy-start(bf16[2,2,128,128]{3,2,1,0:T(8,128)(2,1)S(1)} %collective-permute-done.4.rest_2_) | copy-start | bytes 393220
  33.0 0.7 %copy-start.5 = (bf16[2,2,128,128]{3,2,1,0:T(8,128)(2,1)}, bf16[2,2,128,128]{3,2,1,0:T(8,128)(2,1)S(1)}, u32[]{:S(2)}) copy-start(bf16[2,2,128,128]{3,2,1,0:T(8,128)(2,1)S(1)} %collective-permute-done.5.rest_3_) | copy-start | bytes 393220

commit v3 on v2

--- a/solution.py
+++ b/solution.py
@@ -12,7 +12,6 @@
 VMEM = pl.BlockSpec(memory_space=pltpu.VMEM)
 SMEM = pl.BlockSpec(memory_space=pltpu.SMEM)
 TILE = 256
-FIRST = 16
 
 
 def partner(index, step, groups):
@@ -21,25 +20,30 @@
     return index ^ step, index ^ step
 
 
+def turn_of(index, source, groups):
+    if groups & (groups - 1):
+        return lax.rem(index + groups - source, groups)
+    return index ^ source
+
+
 def fetch_kernel(slots_ref, pool_ref, *rest):
-    *sends, own_ref, sems = rest
+    *sends, token_ref, sems = rest
     groups = slots_ref.shape[2]
     levels = sends[0].shape[0]
     me = lax.axis_index("pool")
     copies = []
-    for step in range(groups - 1, 0, -1):
+    for step in range(groups - 1, -1, -1):
         dest = partner(me, step, groups)[0]
         for level in range(levels):
             slot = slots_ref[dest, level, me]
             copies.append(
                 pltpu.make_async_copy(
-                    pool_ref.at[:, :, slot], sends[step - 1].at[level], sems.at[step, level]
+                    pool_ref.at[:, :, slot], sends[step].at[level], sems.at[step, level]
                 )
             )
     for copy in copies:
         copy.start()
-    for level in range(levels):
-        own_ref[level] = slots_ref[me, level, me]
+    token_ref[0] = me
     for copy in copies:
         copy.wait()
 
@@ -83,9 +87,9 @@
 
 
 def suffix_kernel(
-    scale, per_step, length_ref, start_ref, own_ref, query_ref, suffix_ref, pool_ref, *rest
+    scale, per_step, length_ref, start_ref, _, query_ref, suffix_ref, pool_ref, *rest
 ):
-    mean_ref, log_ref, new_ref, key_ref, page_ref, *back_refs, values, sem = rest
+    mean_ref, log_ref, new_ref, *back_refs, values, sem = rest
     groups = len(back_refs)
     page_len, head_dim = pool_ref.shape[3:]
     suffix = query_ref.shape[0]
@@ -96,7 +100,6 @@
     @pl.when(step == 0)
     def _():
         copy.start()
-        key_ref[0] = suffix_ref[0, 0, pl.ds(0, FIRST), :]
         values[:, pl.ds(0, head_dim)] = suffix_ref[1, 0]
         values[:, pl.ds(head_dim, head_dim)] = jnp.ones((suffix, head_dim), values.dtype)
         me = lax.axis_index("pool")
@@ -106,9 +109,6 @@
             row = pl.multiple_of(jnp.minimum(offset, pages - 1) * page_len, page_len)
             for side in range(2):
                 back_refs[turn][side, 0] = suffix_ref[side, 0, pl.ds(row, page_len), :]
-        for level in range(page_ref.shape[0]):
-            for side in range(2):
-                page_ref[level, side, 0] = pool_ref[side, 0, own_ref[level]]
 
     tile = min(TILE, suffix)
     seen = lax.broadcasted_iota(jnp.int32, (tile, tile), 1) <= lax.broadcasted_iota(
@@ -167,37 +167,44 @@
 
 
 def prefix_kernel(
-    scale, per_step, length_ref, start_ref, query_ref, key_ref, mean_ref, log_ref, *rest
+    scale, per_step, length_ref, start_ref, query_ref, mean_ref, log_ref, *rest
 ):
-    *page_refs, out_ref, keys, values = rest
+    *page_refs, out_ref, token_ref, keys, values = rest
     groups = len(page_refs)
     levels, _, _, page_len, head_dim = page_refs[0].shape
     suffix = query_ref.shape[0]
+
+    token_ref[...] = jnp.zeros_like(token_ref)
 
     @pl.when(pl.program_id(1) == 0)
     def _():
         me = lax.axis_index("pool")
         length, first = length_ref[me], start_ref[me]
+        places = []
         for turn in range(groups):
             owner = partner(me, turn, groups)[1]
             for level in range(levels):
                 rows = pl.ds((turn * levels + level) * page_len, page_len)
                 seen = level * groups + lax.rem(owner + groups - first, groups) < length
+                places.append((rows, seen))
+                keys[rows, :] = page_refs[turn][level, 0, 0]
 
                 @pl.when(seen)
                 def _():
-                    keys[rows, :] = page_refs[turn][level, 0, 0]
                     values[rows, pl.ds(0, head_dim)] = page_refs[turn][level, 1, 0]
                     values[rows, pl.ds(head_dim, head_dim)] = jnp.ones(
                         (page_len, head_dim), values.dtype
                     )
 
-                @pl.when(jnp.logical_not(seen))
-                def _():
-                    keys[rows, :] = jnp.broadcast_to(
-                        key_ref[0, pl.ds(0, 1), :], (page_len, head_dim)
-                    )
-                    values[rows, :] = jnp.zeros((page_len, 2 * head_dim), values.dtype)
+        page_zero = pl.ds(
+            pl.multiple_of(turn_of(me, first, groups) * levels * page_len, page_len), page_len
+        )
+        for rows, seen in places:
+
+            @pl.when(jnp.logical_not(seen))
+            def _():
+                keys[rows, :] = keys[page_zero, :]
+                values[rows, :] = jnp.zeros((page_len, 2 * head_dim), values.dtype)
 
     def scores_of(column):
         query = query_ref[:, pl.ds(column * head_dim, head_dim)]
@@ -241,12 +248,12 @@
             arrived[step - 1] = lax.ppermute(sends[step - 1], "pool", pairs)
         return arrived
 
-    *sends, own_slots = pl.pallas_call(
+    own_pages, *sends, gathered = pl.pallas_call(
         fetch_kernel,
-        out_shape=[pltpu.VMEM((fetched,) + page, dtype)] * (groups - 1)
-        + [jax.ShapeDtypeStruct((fetched,), jnp.int32)],
+        out_shape=[pltpu.VMEM((fetched,) + page, dtype)] * groups
+        + [jax.ShapeDtypeStruct((1,), jnp.int32)],
         in_specs=[SMEM, HBM],
-        out_specs=[VMEM] * (groups - 1) + [SMEM],
+        out_specs=[VMEM] * groups + [SMEM],
         scratch_shapes=[pltpu.SemaphoreType.DMA((groups, fetched))],
         name="gather_pages",
     )(slot_of, pool_kv)
@@ -261,7 +268,6 @@
 
     total = fetched * groups * page_len
     columns = pl.BlockSpec((suffix, per_step * head_dim), lambda h, s: (0, h * steps + s))
-    first_keys = pl.BlockSpec((1, FIRST, head_dim), lambda h, s: (h, 0, 0))
     pages_of = pl.BlockSpec((fetched, 2, 1, page_len, head_dim), lambda h, s: (0, 0, h, 0, 0))
 
     def cost(keys):
@@ -270,15 +276,13 @@
             flops=6 * cells * head_dim, bytes_accessed=8 * queries.size, transcendentals=cells
         )
 
-    means, logs, new_pool, keys, own_pages, own_back, *back_sends = pl.pallas_call(
+    means, logs, new_pool, own_back, *back_sends = pl.pallas_call(
         functools.partial(suffix_kernel, scale, per_step),
         grid=(heads, steps),
         out_shape=[
             jax.ShapeDtypeStruct(queries.shape, jnp.float32),
             jax.ShapeDtypeStruct(queries.shape, jnp.float32),
             jax.ShapeDtypeStruct(pool_kv.shape, dtype),
-            jax.ShapeDtypeStruct((heads, FIRST, head_dim), dtype),
-            jax.ShapeDtypeStruct((fetched,) + page, dtype),
         ]
         + [jax.ShapeDtypeStruct(page, dtype)] * groups,
         in_specs=[
@@ -289,7 +293,7 @@
             pl.BlockSpec((2, 1, suffix, head_dim), lambda h, s: (0, h, 0, 0)),
             pl.BlockSpec((2, 1, slots, page_len, head_dim), lambda h, s: (0, h, 0, 0, 0)),
         ],
-        out_specs=[columns, columns, HBM, first_keys, pages_of]
+        out_specs=[columns, columns, HBM]
         + [pl.BlockSpec((2, 1, page_len, head_dim), lambda h, s: (0, h, 0, 0))] * groups,
         scratch_shapes=[
             pltpu.VMEM((suffix, 2 * head_dim), dtype),
@@ -298,31 +302,33 @@
         compiler_params=grant(60),
         cost_estimate=cost(suffix),
         name="attend_suffix",
-    )(prefix_pages, owner_start, own_slots, queries, suffix_kv, pool_kv)
+    )(prefix_pages, owner_start, gathered, queries, suffix_kv, pool_kv)
     returned = exchange(back_sends)
 
-    result = pl.pallas_call(
+    result, token = pl.pallas_call(
         functools.partial(prefix_kernel, scale, per_step),
         grid=(heads, steps),
-        out_shape=jax.ShapeDtypeStruct(queries.shape, dtype),
+        out_shape=[
+            jax.ShapeDtypeStruct(queries.shape, dtype),
+            jax.ShapeDtypeStruct((8, head_dim), jnp.float32),
+        ],
         in_specs=[
             SMEM,
             SMEM,
-            columns,
-            first_keys,
             columns,
             columns,
+            columns,
         ]
         + [pages_of] * groups,
-        out_specs=columns,
+        out_specs=[columns, pl.BlockSpec((8, head_dim), lambda h, s: (0, 0))],
         scratch_shapes=[
             pltpu.VMEM((total, head_dim), dtype),
             pltpu.VMEM((total, 2 * head_dim), dtype),
         ],
-        compiler_params=grant(60),
+        compiler_params=grant(52),
         cost_estimate=cost(total),
         name="attend_prefix",
-    )(prefix_pages, owner_start, queries, keys, means, logs, own_pages, *received)
+    )(prefix_pages, owner_start, queries, means, logs, own_pages, *received)
 
     new_pool = pl.pallas_call(
         functools.partial(place_kernel, pages),
@@ -331,9 +337,9 @@
         out_specs=HBM,
         input_output_aliases={4 + groups: 0},
         scratch_shapes=[pltpu.SemaphoreType.DMA((groups,))],
-        compiler_params=grant(60),
+        compiler_params=grant(50),
         name="place_pages",
-    )(prefix_pages, owner_start, slot_of, own_back, *returned, result, new_pool)
+    )(prefix_pages, owner_start, slot_of, own_back, *returned, token, new_pool)
     return (result, new_pool)
 
 

time: 36.1 us -> 34.2 us (0.947)
  local copies, waits for them, and re-layouts: 1.44 us -> 0.02 us
  Pallas kernels: 23.4 us -> 23 us
    unnamed x12 -> x8, local copies, waits for them, and re-layouts: 1.44 us -> 0.02 us
    pallas_call x1, Pallas kernels: 1.95 us -> 1.46 us  [body(): pl.pallas_call(functools.partial(place_kernel, pages), out_shape=jax.Shap...]
  transfers between devices with their start and end apart: 6 -> 6, of which waited for: 0 -> 0; matrix products, arithmetic and copies ran while one was open for 0% -> 0% of each run, Pallas kernels for 54% -> 57%
where the time goes in v3:
time: 34.2 us; the launch traced here: 33.9 us
  Pallas kernels  23 us (67%)
  starting transfers between devices  10.1 us (30%)
  between operations  0.71 us (2%)
    ppermute x6, starting transfers between devices, exchange(): arrived[step - 1] = lax.ppermute(sends[step - 1], 'pool', pairs)  10.1 us
    pallas_call x1, Pallas kernels, body(): pl.pallas_call(functools.partial(prefix_kernel, scale, per_step), grid=(h...  9.6 us
    pallas_call x1, Pallas kernels, body(): pl.pallas_call(functools.partial(suffix_kernel, scale, per_step), grid=(h...  9.57 us
    pallas_call x1, Pallas kernels, body(): pl.pallas_call(fetch_kernel, out_shape=[pltpu.VMEM((fetched,) + page, dty...  2.39 us
    pallas_call x1, Pallas kernels, body(): pl.pallas_call(functools.partial(place_kernel, pages), out_shape=jax.Shap...  1.46 us
  transfers between devices with their start and end apart: 6, of which 0 were waited for; matrix products, arithmetic and copies ran while one was open for 0% of the time, Pallas kernels for 57%

profile of v3, /device:TPU:0, one launch (start us, length us, event | category | flops | bytes accessed | tf_op | source)
XLA Modules:
  0.0 33.9 jit_solution(2004324323459333434)
XLA Ops:
  0.6 2.4 %gather_pages.1 = (bf16[1,2,2,128,128]{4,3,2,1,0:T(8,128)(2,1)S(1)}, bf16[1,2,2,128,128]{4,3,2,1,0:T(8,128)(2,1)S(1)}, bf16[1,2,2,128,128]{4,3,2,1,0:T(8,128)(2,...) custom-call(s32[4,2,4]{2,1,0:T(2,128)} %bitcast.1, bf16[2,2,8,128,128]{4,3,2,1,0:T(8,128)(2,1)} %pool_ref.3), custom_call_target="tpu_custom_call" | custom-call | tf_op jit(solution)/shard_map/gather_pages/pallas_call | solution.py:251
  3.0 3.1 %collective-permute-start = (bf16[1,2,2,128,128]{4,3,2,1,0:T(8,128)(2,1)S(1)}, bf16[1,2,2,128,128]{4,3,2,1,0:T(8,128)(2,1)S(1)}, u32[]{:S(2)}, u32[]{:S(2)}) collective-permute-start(bf16[1,2,2,128,128]{4,3,2,1,0:T(8,128)(2,1)S(1)} %get-tuple-element.20), channel_id=1, source_target_pairs={{0,4},{4,0},{8,12},{12,8},{1,5},{5,1},{9,13},{13,9},{2,6},{6,2},{1... | collective-permute-start | bytes 393224 | tf_op jit(solution)/shard_map/ppermute | solution.py:248
  6.1 2.6 %collective-permute-start.1 = (bf16[1,2,2,128,128]{4,3,2,1,0:T(8,128)(2,1)S(1)}, bf16[1,2,2,128,128]{4,3,2,1,0:T(8,128)(2,1)S(1)}, u32[]{:S(2)}, u32[]{:S(2)}) collective-permute-start(bf16[1,2,2,128,128]{4,3,2,1,0:T(8,128)(2,1)S(1)} %get-tuple-element.21), channel_id=1, source_target_pairs={{0,8},{4,12},{8,0},{12,4},{1,9},{5,13},{9,1},{13,5},{2,10},{6,14},... | collective-permute-start | bytes 393224 | tf_op jit(solution)/shard_map/ppermute | solution.py:248
  8.7 0.0 collective-permute-start.2
  8.7 0.0 copy-start.2
  8.7 0.0 copy-start.3
  8.7 9.6 %attend_suffix.1 = (f32[512,2048]{1,0:T(8,128)}, f32[512,2048]{1,0:T(8,128)}, bf16[2,2,8,128,128]{4,3,2,1,0:T(8,128)(2,1)}, bf16[2,2,128,128]{3,2,1,0:T(8,128)(2...) custom-call(s32[4]{0:T(128)} %length_ref.5, ...), custom_call_target="tpu_custom_call" | custom-call | flops 3221225472 | bytes 8388608 | tf_op jit(solution)/shard_map/attend_suffix/pallas_call | solution.py:279
  18.3 1.0 %collective-permute-start.3 = (bf16[2,2,128,128]{3,2,1,0:T(8,128)(2,1)}, bf16[2,2,128,128]{3,2,1,0:T(8,128)(2,1)S(1)}, u32[]{:S(2)}, u32[]{:S(2)}) collective-permute-start(bf16[2,2,128,128]{3,2,1,0:T(8,128)(2,1)} %get-tuple-element.25), channel_id=1, source_target_pairs={{0,4},{4,0},{8,12},{12,8},{1,5},{5,1},{9,13},{13,9},{2,6},{6,2},{1... | collective-permute-start | bytes 393224 | tf_op jit(solution)/shard_map/ppermute | solution.py:248
  19.2 3.5 %collective-permute-start.4 = (bf16[2,2,128,128]{3,2,1,0:T(8,128)(2,1)}, bf16[2,2,128,128]{3,2,1,0:T(8,128)(2,1)S(1)}, u32[]{:S(2)}, u32[]{:S(2)}) collective-permute-start(bf16[2,2,128,128]{3,2,1,0:T(8,128)(2,1)} %get-tuple-element.26), channel_id=1, source_target_pairs={{0,8},{4,12},{8,0},{12,4},{1,9},{5,13},{9,1},{13,5},{2,10},{6,14},... | collective-permute-start | bytes 393224 | tf_op jit(solution)/shard_map/ppermute | solution.py:248
  22.7 0.0 collective-permute-done.rest_1_
  22.7 0.0 collective-permute-start.5
  22.7 0.0 collective-permute-done.1.rest_2_
  22.7 0.0 collective-permute-done.2.rest_3_
  22.8 0.0 copy-done.2
  22.8 0.0 copy-done.3
  22.8 0.0 copy-start
  22.8 0.0 copy-start.1
  22.8 9.6 %attend_prefix.1 = (bf16[512,2048]{1,0:T(8,128)(2,1)}, f32[8,128]{1,0:T(8,128)S(1)}) custom-call(s32[4]{0:T(128)S(1)} %copy-done.2, s32[4]{0:T(128)S(1)} %copy-done.3, bf16[512,2048]{1,0:T(8,128)(2,1)} %query_ref.3, f32[512,2048]{1,0:T(8,128)} %get-tuple-element.17.mean_ref, f32[512,2048]{1,0:T(8,128)} %get-tuple-element.18.log_ref, ...), custom_call_target="tpu_custom_call" | custom-call | flops 3221225472 | bytes 8388608 | tf_op jit(solution)/shard_map/attend_prefix/pallas_call | solution.py:308
  32.4 0.0 collective-permute-done.3.rest_1_
  32.4 0.0 collective-permute-done.4.rest_2_
  32.4 0.0 collective-permute-done.5.rest_3_
  32.4 0.0 copy-done
  32.4 0.0 copy-done.1
  32.4 1.5 %place_pages.1 = bf16[2,2,8,128,128]{4,3,2,1,0:T(8,128)(2,1)} custom-call(s32[4]{0:T(128)S(1)} %copy-done.2, s32[4]{0:T(128)S(1)} %copy-done.3, s32[4,2,4]{2,1,0:T(2,128)S(1)} %bitcast.2, bf16[2,2,128,128]{3,2,1,0:T(8,128)(2,1)S(1)} %copy-done, bf16[2,2,128,128]{3,2,1,0:T(8,128)(2,1)S(1)} %collective-permute-done.3.rest_1_, ...), custom_call_target="tpu_custom_call", output_to_operand_aliasing={{}: (8, {})} | custom-call | tf_op jit(solution)/shard_map/place_pages/pallas_call | solution.py:333
Async XLA Ops:
  3.0 19.7 %collective-permute-start = (bf16[1,2,2,128,128]{4,3,2,1,0:T(8,128)(2,1)S(1)}, bf16[1,2,2,128,128]{4,3,2,1,0:T(8,128)(2,1)S(1)}, u32[]{:S(2)}, u32[]{:S(2)}) collective-permute-start(bf16[1,2,2,128,128]{4,3,2,1,0:T(8,128)(2,1)S(1)} %get-tuple-element.20), channel_id=1, source_target_pairs={{0,4},{4,0},{8,12},{12,8},{1,5},{5,1},{9,13},{13,9},{2,6},{6,2},{1... | collective-permute-start | bytes 393224 | tf_op jit(solution)/shard_map/ppermute | solution.py:248
  6.1 16.6 %collective-permute-start.1 = (bf16[1,2,2,128,128]{4,3,2,1,0:T(8,128)(2,1)S(1)}, bf16[1,2,2,128,128]{4,3,2,1,0:T(8,128)(2,1)S(1)}, u32[]{:S(2)}, u32[]{:S(2)}) collective-permute-start(bf16[1,2,2,128,128]{4,3,2,1,0:T(8,128)(2,1)S(1)} %get-tuple-element.21), channel_id=1, source_target_pairs={{0,8},{4,12},{8,0},{12,4},{1,9},{5,13},{9,1},{13,5},{2,10},{6,14},... | collective-permute-start | bytes 393224 | tf_op jit(solution)/shard_map/ppermute | solution.py:248
  8.7 14.0 %collective-permute-start.2 = (bf16[1,2,2,128,128]{4,3,2,1,0:T(8,128)(2,1)S(1)}, bf16[1,2,2,128,128]{4,3,2,1,0:T(8,128)(2,1)S(1)}, u32[]{:S(2)}, u32[]{:S(2)}) collective-permute-start(bf16[1,2,2,128,128]{4,3,2,1,0:T(8,128)(2,1)S(1)} %get-tuple-element.22), channel_id=1, source_target_pairs={{0,12},{4,8},{8,4},{12,0},{1,13},{5,9},{9,5},{13,1},{2,14},{6,10},... | collective-permute-start | bytes 393224 | tf_op jit(solution)/shard_map/ppermute | solution.py:248
  8.7 14.1 %copy-start.2 = (s32[4]{0:T(128)S(1)}, s32[4]{0:T(128)}, u32[]{:S(2)}) copy-start(s32[4]{0:T(128)} %length_ref.5) | copy-start | bytes 52
  8.7 14.1 %copy-start.3 = (s32[4]{0:T(128)S(1)}, s32[4]{0:T(128)}, u32[]{:S(2)}) copy-start(s32[4]{0:T(128)} %start_ref.5) | copy-start | bytes 52
  18.3 14.1 %collective-permute-start.3 = (bf16[2,2,128,128]{3,2,1,0:T(8,128)(2,1)}, bf16[2,2,128,128]{3,2,1,0:T(8,128)(2,1)S(1)}, u32[]{:S(2)}, u32[]{:S(2)}) collective-permute-start(bf16[2,2,128,128]{3,2,1,0:T(8,128)(2,1)} %get-tuple-element.25), channel_id=1, source_target_pairs={{0,4},{4,0},{8,12},{12,8},{1,5},{5,1},{9,13},{13,9},{2,6},{6,2},{1... | collective-permute-start | bytes 393224 | tf_op jit(solution)/shard_map/ppermute | solution.py:248
  19.2 13.2 %collective-permute-start.4 = (bf16[2,2,128,128]{3,2,1,0:T(8,128)(2,1)}, bf16[2,2,128,128]{3,2,1,0:T(8,128)(2,1)S(1)}, u32[]{:S(2)}, u32[]{:S(2)}) collective-permute-start(bf16[2,2,128,128]{3,2,1,0:T(8,128)(2,1)} %get-tuple-element.26), channel_id=1, source_target_pairs={{0,8},{4,12},{8,0},{12,4},{1,9},{5,13},{9,1},{13,5},{2,10},{6,14},... | collective-permute-start | bytes 393224 | tf_op jit(solution)/shard_map/ppermute | solution.py:248
  22.7 9.7 %collective-permute-start.5 = (bf16[2,2,128,128]{3,2,1,0:T(8,128)(2,1)}, bf16[2,2,128,128]{3,2,1,0:T(8,128)(2,1)S(1)}, u32[]{:S(2)}, u32[]{:S(2)}) collective-permute-start(bf16[2,2,128,128]{3,2,1,0:T(8,128)(2,1)} %get-tuple-element.27), channel_id=1, source_target_pairs={{0,12},{4,8},{8,4},{12,0},{1,13},{5,9},{9,5},{13,1},{2,14},{6,10},... | collective-permute-start | bytes 393224 | tf_op jit(solution)/shard_map/ppermute | solution.py:248
  22.8 9.6 %copy-start = (bf16[2,2,128,128]{3,2,1,0:T(8,128)(2,1)S(1)}, bf16[2,2,128,128]{3,2,1,0:T(8,128)(2,1)}, u32[]{:S(2)}) copy-start(bf16[2,2,128,128]{3,2,1,0:T(8,128)(2,1)} %get-tuple-element.24.rest_0_) | copy-start | bytes 393220
  22.8 9.6 %copy-start.1 = (s32[4,4,2]{1,2,0:T(2,128)S(1)}, s32[4,4,2]{1,2,0:T(2,128)}, u32[]{:S(2)}) copy-start(s32[4,4,2]{1,2,0:T(2,128)} %param.11) | copy-start | bytes 388

commit v4 on v3

--- a/solution.py
+++ b/solution.py
@@ -259,7 +259,7 @@
     )(slot_of, pool_kv)
     received = exchange(sends)
 
-    per_step = math.gcd(per_kv, 4)
+    per_step = math.gcd(per_kv, 2)
     steps = per_kv // per_step
     scale = math.log2(math.e) / math.sqrt(head_dim)
 

time: 34.2 us -> 38.2 us (1.12)
  Pallas kernels: 23 us -> 26.8 us
    pallas_call x1, Pallas kernels: 9.6 us -> 11.6 us  [body(): pl.pallas_call(functools.partial(prefix_kernel, scale, per_step), grid=(h...]
    pallas_call x1, Pallas kernels: 9.57 us -> 11.3 us  [body(): pl.pallas_call(functools.partial(suffix_kernel, scale, per_step), grid=(h...]
  transfers between devices with their start and end apart: 6 -> 6, of which waited for: 0 -> 0; matrix products, arithmetic and copies ran while one was open for 0% -> 0% of each run, Pallas kernels for 57% -> 61%
where the time goes in v4:
time: 38.2 us; the launch traced here: 37.7 us
  Pallas kernels  26.8 us (70%)
  starting transfers between devices  10.1 us (26%)
  between operations  0.72 us (2%)
    pallas_call x1, Pallas kernels, body(): pl.pallas_call(functools.partial(prefix_kernel, scale, per_step), grid=(h...  11.6 us
    pallas_call x1, Pallas kernels, body(): pl.pallas_call(functools.partial(suffix_kernel, scale, per_step), grid=(h...  11.3 us
    ppermute x6, starting transfers between devices, exchange(): arrived[step - 1] = lax.ppermute(sends[step - 1], 'pool', pairs)  10.1 us
    pallas_call x1, Pallas kernels, body(): pl.pallas_call(fetch_kernel, out_shape=[pltpu.VMEM((fetched,) + page, dty...  2.39 us
    pallas_call x1, Pallas kernels, body(): pl.pallas_call(functools.partial(place_kernel, pages), out_shape=jax.Shap...  1.46 us
  transfers between devices with their start and end apart: 6, of which 0 were waited for; matrix products, arithmetic and copies ran while one was open for 0% of the time, Pallas kernels for 61%

profile of v4, /device:TPU:0, one launch (start us, length us, event | category | flops | bytes accessed | tf_op | source)
XLA Modules:
  0.0 37.7 jit_solution(12383570404489204257)
XLA Ops:
  0.6 2.4 %gather_pages.1 = (bf16[1,2,2,128,128]{4,3,2,1,0:T(8,128)(2,1)S(1)}, bf16[1,2,2,128,128]{4,3,2,1,0:T(8,128)(2,1)S(1)}, bf16[1,2,2,128,128]{4,3,2,1,0:T(8,128)(2,...) custom-call(s32[4,2,4]{2,1,0:T(2,128)} %bitcast.1, bf16[2,2,8,128,128]{4,3,2,1,0:T(8,128)(2,1)} %pool_ref.3), custom_call_target="tpu_custom_call" | custom-call | tf_op jit(solution)/shard_map/gather_pages/pallas_call | solution.py:251
  3.0 3.1 %collective-permute-start = (bf16[1,2,2,128,128]{4,3,2,1,0:T(8,128)(2,1)S(1)}, bf16[1,2,2,128,128]{4,3,2,1,0:T(8,128)(2,1)S(1)}, u32[]{:S(2)}, u32[]{:S(2)}) collective-permute-start(bf16[1,2,2,128,128]{4,3,2,1,0:T(8,128)(2,1)S(1)} %get-tuple-element.20), channel_id=1, source_target_pairs={{0,4},{4,0},{8,12},{12,8},{1,5},{5,1},{9,13},{13,9},{2,6},{6,2},{1... | collective-permute-start | bytes 393224 | tf_op jit(solution)/shard_map/ppermute | solution.py:248
  6.1 2.6 %collective-permute-start.1 = (bf16[1,2,2,128,128]{4,3,2,1,0:T(8,128)(2,1)S(1)}, bf16[1,2,2,128,128]{4,3,2,1,0:T(8,128)(2,1)S(1)}, u32[]{:S(2)}, u32[]{:S(2)}) collective-permute-start(bf16[1,2,2,128,128]{4,3,2,1,0:T(8,128)(2,1)S(1)} %get-tuple-element.21), channel_id=1, source_target_pairs={{0,8},{4,12},{8,0},{12,4},{1,9},{5,13},{9,1},{13,5},{2,10},{6,14},... | collective-permute-start | bytes 393224 | tf_op jit(solution)/shard_map/ppermute | solution.py:248
  8.7 0.0 collective-permute-start.2
  8.7 0.0 copy-start.2
  8.7 0.0 copy-start.3
  8.7 11.3 %attend_suffix.1 = (f32[512,2048]{1,0:T(8,128)}, f32[512,2048]{1,0:T(8,128)}, bf16[2,2,8,128,128]{4,3,2,1,0:T(8,128)(2,1)}, bf16[2,2,128,128]{3,2,1,0:T(8,128)(2...) custom-call(s32[4]{0:T(128)} %length_ref.5, ...), custom_call_target="tpu_custom_call" | custom-call | flops 3221225472 | bytes 8388608 | tf_op jit(solution)/shard_map/attend_suffix/pallas_call | solution.py:279
  20.1 1.0 %collective-permute-start.3 = (bf16[2,2,128,128]{3,2,1,0:T(8,128)(2,1)}, bf16[2,2,128,128]{3,2,1,0:T(8,128)(2,1)S(1)}, u32[]{:S(2)}, u32[]{:S(2)}) collective-permute-start(bf16[2,2,128,128]{3,2,1,0:T(8,128)(2,1)} %get-tuple-element.25), channel_id=1, source_target_pairs={{0,4},{4,0},{8,12},{12,8},{1,5},{5,1},{9,13},{13,9},{2,6},{6,2},{1... | collective-permute-start | bytes 393224 | tf_op jit(solution)/shard_map/ppermute | solution.py:248
  21.0 3.5 %collective-permute-start.4 = (bf16[2,2,128,128]{3,2,1,0:T(8,128)(2,1)}, bf16[2,2,128,128]{3,2,1,0:T(8,128)(2,1)S(1)}, u32[]{:S(2)}, u32[]{:S(2)}) collective-permute-start(bf16[2,2,128,128]{3,2,1,0:T(8,128)(2,1)} %get-tuple-element.26), channel_id=1, source_target_pairs={{0,8},{4,12},{8,0},{12,4},{1,9},{5,13},{9,1},{13,5},{2,10},{6,14},... | collective-permute-start | bytes 393224 | tf_op jit(solution)/shard_map/ppermute | solution.py:248
  24.5 0.0 collective-permute-done.rest_1_
  24.5 0.0 collective-permute-start.5
  24.5 0.0 collective-permute-done.1.rest_2_
  24.5 0.0 collective-permute-done.2.rest_3_
  24.5 0.0 copy-done.2
  24.5 0.0 copy-done.3
  24.6 0.0 copy-start
  24.6 0.0 copy-start.1
  24.6 11.6 %attend_prefix.1 = (bf16[512,2048]{1,0:T(8,128)(2,1)}, f32[8,128]{1,0:T(8,128)S(1)}) custom-call(s32[4]{0:T(128)S(1)} %copy-done.2, s32[4]{0:T(128)S(1)} %copy-done.3, bf16[512,2048]{1,0:T(8,128)(2,1)} %query_ref.3, f32[512,2048]{1,0:T(8,128)} %get-tuple-element.17.mean_ref, f32[512,2048]{1,0:T(8,128)} %get-tuple-element.18.log_ref, ...), custom_call_target="tpu_custom_call" | custom-call | flops 3221225472 | bytes 8388608 | tf_op jit(solution)/shard_map/attend_prefix/pallas_call | solution.py:308
  36.2 0.0 collective-permute-done.3.rest_1_
  36.2 0.0 collective-permute-done.4.rest_2_
  36.2 0.0 collective-permute-done.5.rest_3_
  36.2 0.0 copy-done
  36.2 0.0 copy-done.1
  36.2 1.5 %place_pages.1 = bf16[2,2,8,128,128]{4,3,2,1,0:T(8,128)(2,1)} custom-call(s32[4]{0:T(128)S(1)} %copy-done.2, s32[4]{0:T(128)S(1)} %copy-done.3, s32[4,2,4]{2,1,0:T(2,128)S(1)} %bitcast.2, bf16[2,2,128,128]{3,2,1,0:T(8,128)(2,1)S(1)} %copy-done, bf16[2,2,128,128]{3,2,1,0:T(8,128)(2,1)S(1)} %collective-permute-done.3.rest_1_, ...), custom_call_target="tpu_custom_call", output_to_operand_aliasing={{}: (8, {})} | custom-call | tf_op jit(solution)/shard_map/place_pages/pallas_call | solution.py:333
Async XLA Ops:
  3.0 21.5 %collective-permute-start = (bf16[1,2,2,128,128]{4,3,2,1,0:T(8,128)(2,1)S(1)}, bf16[1,2,2,128,128]{4,3,2,1,0:T(8,128)(2,1)S(1)}, u32[]{:S(2)}, u32[]{:S(2)}) collective-permute-start(bf16[1,2,2,128,128]{4,3,2,1,0:T(8,128)(2,1)S(1)} %get-tuple-element.20), channel_id=1, source_target_pairs={{0,4},{4,0},{8,12},{12,8},{1,5},{5,1},{9,13},{13,9},{2,6},{6,2},{1... | collective-permute-start | bytes 393224 | tf_op jit(solution)/shard_map/ppermute | solution.py:248
  6.1 18.4 %collective-permute-start.1 = (bf16[1,2,2,128,128]{4,3,2,1,0:T(8,128)(2,1)S(1)}, bf16[1,2,2,128,128]{4,3,2,1,0:T(8,128)(2,1)S(1)}, u32[]{:S(2)}, u32[]{:S(2)}) collective-permute-start(bf16[1,2,2,128,128]{4,3,2,1,0:T(8,128)(2,1)S(1)} %get-tuple-element.21), channel_id=1, source_target_pairs={{0,8},{4,12},{8,0},{12,4},{1,9},{5,13},{9,1},{13,5},{2,10},{6,14},... | collective-permute-start | bytes 393224 | tf_op jit(solution)/shard_map/ppermute | solution.py:248
  8.7 15.8 %collective-permute-start.2 = (bf16[1,2,2,128,128]{4,3,2,1,0:T(8,128)(2,1)S(1)}, bf16[1,2,2,128,128]{4,3,2,1,0:T(8,128)(2,1)S(1)}, u32[]{:S(2)}, u32[]{:S(2)}) collective-permute-start(bf16[1,2,2,128,128]{4,3,2,1,0:T(8,128)(2,1)S(1)} %get-tuple-element.22), channel_id=1, source_target_pairs={{0,12},{4,8},{8,4},{12,0},{1,13},{5,9},{9,5},{13,1},{2,14},{6,10},... | collective-permute-start | bytes 393224 | tf_op jit(solution)/shard_map/ppermute | solution.py:248
  8.7 15.8 %copy-start.2 = (s32[4]{0:T(128)S(1)}, s32[4]{0:T(128)}, u32[]{:S(2)}) copy-start(s32[4]{0:T(128)} %length_ref.5) | copy-start | bytes 52
  8.7 15.8 %copy-start.3 = (s32[4]{0:T(128)S(1)}, s32[4]{0:T(128)}, u32[]{:S(2)}) copy-start(s32[4]{0:T(128)} %start_ref.5) | copy-start | bytes 52
  20.1 16.1 %collective-permute-start.3 = (bf16[2,2,128,128]{3,2,1,0:T(8,128)(2,1)}, bf16[2,2,128,128]{3,2,1,0:T(8,128)(2,1)S(1)}, u32[]{:S(2)}, u32[]{:S(2)}) collective-permute-start(bf16[2,2,128,128]{3,2,1,0:T(8,128)(2,1)} %get-tuple-element.25), channel_id=1, source_target_pairs={{0,4},{4,0},{8,12},{12,8},{1,5},{5,1},{9,13},{13,9},{2,6},{6,2},{1... | collective-permute-start | bytes 393224 | tf_op jit(solution)/shard_map/ppermute | solution.py:248
  21.0 15.1 %collective-permute-start.4 = (bf16[2,2,128,128]{3,2,1,0:T(8,128)(2,1)}, bf16[2,2,128,128]{3,2,1,0:T(8,128)(2,1)S(1)}, u32[]{:S(2)}, u32[]{:S(2)}) collective-permute-start(bf16[2,2,128,128]{3,2,1,0:T(8,128)(2,1)} %get-tuple-element.26), channel_id=1, source_target_pairs={{0,8},{4,12},{8,0},{12,4},{1,9},{5,13},{9,1},{13,5},{2,10},{6,14},... | collective-permute-start | bytes 393224 | tf_op jit(solution)/shard_map/ppermute | solution.py:248
  24.5 11.7 %collective-permute-start.5 = (bf16[2,2,128,128]{3,2,1,0:T(8,128)(2,1)}, bf16[2,2,128,128]{3,2,1,0:T(8,128)(2,1)S(1)}, u32[]{:S(2)}, u32[]{:S(2)}) collective-permute-start(bf16[2,2,128,128]{3,2,1,0:T(8,128)(2,1)} %get-tuple-element.27), channel_id=1, source_target_pairs={{0,12},{4,8},{8,4},{12,0},{1,13},{5,9},{9,5},{13,1},{2,14},{6,10},... | collective-permute-start | bytes 393224 | tf_op jit(solution)/shard_map/ppermute | solution.py:248
  24.6 11.6 %copy-start = (bf16[2,2,128,128]{3,2,1,0:T(8,128)(2,1)S(1)}, bf16[2,2,128,128]{3,2,1,0:T(8,128)(2,1)}, u32[]{:S(2)}) copy-start(bf16[2,2,128,128]{3,2,1,0:T(8,128)(2,1)} %get-tuple-element.24.rest_0_) | copy-start | bytes 393220
  24.6 11.6 %copy-start.1 = (s32[4,4,2]{1,2,0:T(2,128)S(1)}, s32[4,4,2]{1,2,0:T(2,128)}, u32[]{:S(2)}) copy-start(s32[4,4,2]{1,2,0:T(2,128)} %param.11) | copy-start | bytes 388

commit v5 on v3

--- a/solution.py
+++ b/solution.py
@@ -89,13 +89,30 @@
 def suffix_kernel(
     scale, per_step, length_ref, start_ref, _, query_ref, suffix_ref, pool_ref, *rest
 ):
-    mean_ref, log_ref, new_ref, *back_refs, values, sem = rest
+    mean_out, log_out, new_ref, *back_refs, means, logs, values, sem, sems = rest
     groups = len(back_refs)
     page_len, head_dim = pool_ref.shape[3:]
     suffix = query_ref.shape[0]
     pages = suffix // page_len
     head, step = pl.program_id(0), pl.program_id(1)
     copy = pltpu.make_async_copy(pool_ref, new_ref.at[:, pl.ds(head, 1)], sem)
+    turn_now = head * pl.num_programs(1) + step
+
+    def leaving(column):
+        place = step * per_step + column
+        return [
+            pltpu.make_async_copy(means.at[column], mean_out.at[head, place], sems.at[0, column]),
+            pltpu.make_async_copy(logs.at[column], log_out.at[head, place], sems.at[1, column]),
+        ]
+
+    def wait_leaving():
+        for column in range(per_step):
+            for part in leaving(column):
+                part.wait()
+
+    @pl.when(turn_now > 0)
+    def _():
+        wait_leaving()
 
     @pl.when(step == 0)
     def _():
@@ -123,7 +140,6 @@
         ]
 
     def finish(column, scores):
-        lanes = pl.ds(column * head_dim, head_dim)
         scores = [
             [
                 block[row : row + tile] if row else jnp.where(seen, block[:tile], -jnp.inf)
@@ -156,14 +172,20 @@
         for row in range(blocks):
             rows = pl.ds(row * tile, tile)
             count = mixed[row][:, head_dim:]
-            mean_ref[rows, lanes] = mixed[row][:, :head_dim] / count
-            log_ref[rows, lanes] = tops[row] * scale + jnp.log2(count)
+            means[column, rows, :] = mixed[row][:, :head_dim] / count
+            logs[column, rows, :] = tops[row] * scale + jnp.log2(count)
+        for part in leaving(column):
+            part.start()
 
     staggered(range(per_step), scores_of, finish)
 
     @pl.when(step == pl.num_programs(1) - 1)
     def _():
         copy.wait()
+
+    @pl.when(turn_now == pl.num_programs(0) * pl.num_programs(1) - 1)
+    def _():
+        wait_leaving()
 
 
 def prefix_kernel(
@@ -212,7 +234,7 @@
 
     def finish(column, score):
         lanes = pl.ds(column * head_dim, head_dim)
-        before = log_ref[:, lanes]
+        before = log_ref[0, column]
         top = jnp.maximum(before, jnp.max(score, axis=1, keepdims=True) * scale)
         weight = jnp.concatenate(
             [
@@ -224,7 +246,7 @@
         mixed = dot(weight, values[...], ALONG)
         share = jnp.exp2(before - top)
         out_ref[:, lanes] = (
-            (mixed[:, :head_dim] + mean_ref[:, lanes] * share) / (mixed[:, head_dim:] + share)
+            (mixed[:, :head_dim] + mean_ref[0, column] * share) / (mixed[:, head_dim:] + share)
         ).astype(out_ref.dtype)
 
     staggered(range(per_step), scores_of, finish)
@@ -268,6 +290,7 @@
 
     total = fetched * groups * page_len
     columns = pl.BlockSpec((suffix, per_step * head_dim), lambda h, s: (0, h * steps + s))
+    per_head = pl.BlockSpec((1, per_step, suffix, head_dim), lambda h, s: (h, s, 0, 0))
     pages_of = pl.BlockSpec((fetched, 2, 1, page_len, head_dim), lambda h, s: (0, 0, h, 0, 0))
 
     def cost(keys):
@@ -277,11 +300,11 @@
         )
 
     means, logs, new_pool, own_back, *back_sends = pl.pallas_call(
-        functools.partial(suffix_kernel, scale, per_step),
-        grid=(heads, steps),
+        functools.partial(suffix_kernel, scale, per_kv),
+        grid=(heads, 1),
         out_shape=[
-            jax.ShapeDtypeStruct(queries.shape, jnp.float32),
-            jax.ShapeDtypeStruct(queries.shape, jnp.float32),
+            jax.ShapeDtypeStruct((heads, per_kv, suffix, head_dim), jnp.float32),
+            jax.ShapeDtypeStruct((heads, per_kv, suffix, head_dim), jnp.float32),
             jax.ShapeDtypeStruct(pool_kv.shape, dtype),
         ]
         + [jax.ShapeDtypeStruct(page, dtype)] * groups,
@@ -289,15 +312,18 @@
             SMEM,
             SMEM,
             SMEM,
-            columns,
+            pl.BlockSpec((suffix, per_kv * head_dim), lambda h, s: (0, h)),
             pl.BlockSpec((2, 1, suffix, head_dim), lambda h, s: (0, h, 0, 0)),
             pl.BlockSpec((2, 1, slots, page_len, head_dim), lambda h, s: (0, h, 0, 0, 0)),
         ],
-        out_specs=[columns, columns, HBM]
+        out_specs=[HBM, HBM, HBM]
         + [pl.BlockSpec((2, 1, page_len, head_dim), lambda h, s: (0, h, 0, 0))] * groups,
         scratch_shapes=[
+            pltpu.VMEM((per_kv, suffix, head_dim), jnp.float32),
+            pltpu.VMEM((per_kv, suffix, head_dim), jnp.float32),
             pltpu.VMEM((suffix, 2 * head_dim), dtype),
             pltpu.SemaphoreType.DMA(()),
+            pltpu.SemaphoreType.DMA((2, per_kv)),
         ],
         compiler_params=grant(60),
         cost_estimate=cost(suffix),
@@ -316,8 +342,8 @@
             SMEM,
             SMEM,
             columns,
-            columns,
-            columns,
+            per_head,
+            per_head,
         ]
         + [pages_of] * groups,
         out_specs=[columns, pl.BlockSpec((8, head_dim), lambda h, s: (0, 0))],

time: 34.2 us -> 33.9 us (level)
  transfers between devices with their start and end apart: 6 -> 6, of which waited for: 0 -> 0; matrix products, arithmetic and copies ran while one was open for 0% -> 0% of each run, Pallas kernels for 57% -> 56%
where the time goes in v5:
time: 33.9 us; the launch traced here: 33.7 us
  Pallas kernels  22.8 us (67%)
  starting transfers between devices  10.1 us (30%)
  between operations  0.71 us (2%)
    ppermute x6, starting transfers between devices, exchange(): arrived[step - 1] = lax.ppermute(sends[step - 1], 'pool', pairs)  10.1 us
    pallas_call x1, Pallas kernels, body(): pl.pallas_call(functools.partial(prefix_kernel, scale, per_step), grid=(h...  9.57 us
    pallas_call x1, Pallas kernels, body(): pl.pallas_call(functools.partial(suffix_kernel, scale, per_kv), grid=(hea...  9.37 us
    pallas_call x1, Pallas kernels, body(): pl.pallas_call(fetch_kernel, out_shape=[pltpu.VMEM((fetched,) + page, dty...  2.39 us
    pallas_call x1, Pallas kernels, body(): pl.pallas_call(functools.partial(place_kernel, pages), out_shape=jax.Shap...  1.46 us
  transfers between devices with their start and end apart: 6, of which 0 were waited for; matrix products, arithmetic and copies ran while one was open for 0% of the time, Pallas kernels for 56%

profile of v5, /device:TPU:0, one launch (start us, length us, event | category | flops | bytes accessed | tf_op | source)
XLA Modules:
  0.0 33.7 jit_solution(5919813657310867687)
XLA Ops:
  0.6 2.4 %gather_pages.1 = (bf16[1,2,2,128,128]{4,3,2,1,0:T(8,128)(2,1)S(1)}, bf16[1,2,2,128,128]{4,3,2,1,0:T(8,128)(2,1)S(1)}, bf16[1,2,2,128,128]{4,3,2,1,0:T(8,128)(2,...) custom-call(s32[4,2,4]{2,1,0:T(2,128)} %bitcast.1, bf16[2,2,8,128,128]{4,3,2,1,0:T(8,128)(2,1)} %pool_ref.3), custom_call_target="tpu_custom_call" | custom-call | tf_op jit(solution)/shard_map/gather_pages/pallas_call | solution.py:273
  3.0 3.1 %collective-permute-start = (bf16[1,2,2,128,128]{4,3,2,1,0:T(8,128)(2,1)S(1)}, bf16[1,2,2,128,128]{4,3,2,1,0:T(8,128)(2,1)S(1)}, u32[]{:S(2)}, u32[]{:S(2)}) collective-permute-start(bf16[1,2,2,128,128]{4,3,2,1,0:T(8,128)(2,1)S(1)} %get-tuple-element.20), channel_id=1, source_target_pairs={{0,4},{4,0},{8,12},{12,8},{1,5},{5,1},{9,13},{13,9},{2,6},{6,2},{1... | collective-permute-start | bytes 393224 | tf_op jit(solution)/shard_map/ppermute | solution.py:270
  6.1 2.6 %collective-permute-start.1 = (bf16[1,2,2,128,128]{4,3,2,1,0:T(8,128)(2,1)S(1)}, bf16[1,2,2,128,128]{4,3,2,1,0:T(8,128)(2,1)S(1)}, u32[]{:S(2)}, u32[]{:S(2)}) collective-permute-start(bf16[1,2,2,128,128]{4,3,2,1,0:T(8,128)(2,1)S(1)} %get-tuple-element.21), channel_id=1, source_target_pairs={{0,8},{4,12},{8,0},{12,4},{1,9},{5,13},{9,1},{13,5},{2,10},{6,14},... | collective-permute-start | bytes 393224 | tf_op jit(solution)/shard_map/ppermute | solution.py:270
  8.7 0.0 collective-permute-start.2
  8.7 0.0 copy-start.2
  8.7 0.0 copy-start.3
  8.7 9.4 %attend_suffix.1 = (f32[2,8,512,128]{3,2,1,0:T(8,128)}, f32[2,8,512,128]{3,2,1,0:T(8,128)}, bf16[2,2,8,128,128]{4,3,2,1,0:T(8,128)(2,1)}, bf16[2,2,128,128]{3,2,...) custom-call(s32[4]{0:T(128)} %length_ref.5, ...), custom_call_target="tpu_custom_call" | custom-call | flops 3221225472 | bytes 8388608 | tf_op jit(solution)/shard_map/attend_suffix/pallas_call | solution.py:302
  18.1 1.0 %collective-permute-start.3 = (bf16[2,2,128,128]{3,2,1,0:T(8,128)(2,1)}, bf16[2,2,128,128]{3,2,1,0:T(8,128)(2,1)S(1)}, u32[]{:S(2)}, u32[]{:S(2)}) collective-permute-start(bf16[2,2,128,128]{3,2,1,0:T(8,128)(2,1)} %get-tuple-element.25), channel_id=1, source_target_pairs={{0,4},{4,0},{8,12},{12,8},{1,5},{5,1},{9,13},{13,9},{2,6},{6,2},{1... | collective-permute-start | bytes 393224 | tf_op jit(solution)/shard_map/ppermute | solution.py:270
  19.1 3.5 %collective-permute-start.4 = (bf16[2,2,128,128]{3,2,1,0:T(8,128)(2,1)}, bf16[2,2,128,128]{3,2,1,0:T(8,128)(2,1)S(1)}, u32[]{:S(2)}, u32[]{:S(2)}) collective-permute-start(bf16[2,2,128,128]{3,2,1,0:T(8,128)(2,1)} %get-tuple-element.26), channel_id=1, source_target_pairs={{0,8},{4,12},{8,0},{12,4},{1,9},{5,13},{9,1},{13,5},{2,10},{6,14},... | collective-permute-start | bytes 393224 | tf_op jit(solution)/shard_map/ppermute | solution.py:270
  22.5 0.0 collective-permute-done.rest_1_
  22.5 0.0 collective-permute-start.5
  22.5 0.0 collective-permute-done.1.rest_2_
  22.5 0.0 collective-permute-done.2.rest_3_
  22.6 0.0 copy-done.2
  22.6 0.0 copy-done.3
  22.6 0.0 copy-start
  22.6 0.0 copy-start.1
  22.6 9.6 %attend_prefix.1 = (bf16[512,2048]{1,0:T(8,128)(2,1)}, f32[8,128]{1,0:T(8,128)S(1)}) custom-call(s32[4]{0:T(128)S(1)} %copy-done.2, s32[4]{0:T(128)S(1)} %copy-done.3, bf16[512,2048]{1,0:T(8,128)(2,1)} %query_ref.3, f32[2,8,512,128]{3,2,1,0:T(8,128)} %get-tuple-element.17.mean_ref, f32[2,8,512,128]{3,2,1,0:T(8,128)} %get-tuple-element.18.log_ref, ...), custom_call_target="tpu_custom_call" | custom-call | flops 3221225472 | bytes 8388608 | tf_op jit(solution)/shard_map/attend_prefix/pallas_call | solution.py:334
  32.2 0.0 collective-permute-done.3.rest_1_
  32.2 0.0 collective-permute-done.4.rest_2_
  32.2 0.0 collective-permute-done.5.rest_3_
  32.2 0.0 copy-done
  32.2 0.0 copy-done.1
  32.2 1.5 %place_pages.1 = bf16[2,2,8,128,128]{4,3,2,1,0:T(8,128)(2,1)} custom-call(s32[4]{0:T(128)S(1)} %copy-done.2, s32[4]{0:T(128)S(1)} %copy-done.3, s32[4,2,4]{2,1,0:T(2,128)S(1)} %bitcast.2, bf16[2,2,128,128]{3,2,1,0:T(8,128)(2,1)S(1)} %copy-done, bf16[2,2,128,128]{3,2,1,0:T(8,128)(2,1)S(1)} %collective-permute-done.3.rest_1_, ...), custom_call_target="tpu_custom_call", output_to_operand_aliasing={{}: (8, {})} | custom-call | tf_op jit(solution)/shard_map/place_pages/pallas_call | solution.py:359
Async XLA Ops:
  3.0 19.5 %collective-permute-start = (bf16[1,2,2,128,128]{4,3,2,1,0:T(8,128)(2,1)S(1)}, bf16[1,2,2,128,128]{4,3,2,1,0:T(8,128)(2,1)S(1)}, u32[]{:S(2)}, u32[]{:S(2)}) collective-permute-start(bf16[1,2,2,128,128]{4,3,2,1,0:T(8,128)(2,1)S(1)} %get-tuple-element.20), channel_id=1, source_target_pairs={{0,4},{4,0},{8,12},{12,8},{1,5},{5,1},{9,13},{13,9},{2,6},{6,2},{1... | collective-permute-start | bytes 393224 | tf_op jit(solution)/shard_map/ppermute | solution.py:270
  6.1 16.4 %collective-permute-start.1 = (bf16[1,2,2,128,128]{4,3,2,1,0:T(8,128)(2,1)S(1)}, bf16[1,2,2,128,128]{4,3,2,1,0:T(8,128)(2,1)S(1)}, u32[]{:S(2)}, u32[]{:S(2)}) collective-permute-start(bf16[1,2,2,128,128]{4,3,2,1,0:T(8,128)(2,1)S(1)} %get-tuple-element.21), channel_id=1, source_target_pairs={{0,8},{4,12},{8,0},{12,4},{1,9},{5,13},{9,1},{13,5},{2,10},{6,14},... | collective-permute-start | bytes 393224 | tf_op jit(solution)/shard_map/ppermute | solution.py:270
  8.7 13.8 %collective-permute-start.2 = (bf16[1,2,2,128,128]{4,3,2,1,0:T(8,128)(2,1)S(1)}, bf16[1,2,2,128,128]{4,3,2,1,0:T(8,128)(2,1)S(1)}, u32[]{:S(2)}, u32[]{:S(2)}) collective-permute-start(bf16[1,2,2,128,128]{4,3,2,1,0:T(8,128)(2,1)S(1)} %get-tuple-element.22), channel_id=1, source_target_pairs={{0,12},{4,8},{8,4},{12,0},{1,13},{5,9},{9,5},{13,1},{2,14},{6,10},... | collective-permute-start | bytes 393224 | tf_op jit(solution)/shard_map/ppermute | solution.py:270
  8.7 13.8 %copy-start.2 = (s32[4]{0:T(128)S(1)}, s32[4]{0:T(128)}, u32[]{:S(2)}) copy-start(s32[4]{0:T(128)} %length_ref.5) | copy-start | bytes 52
  8.7 13.9 %copy-start.3 = (s32[4]{0:T(128)S(1)}, s32[4]{0:T(128)}, u32[]{:S(2)}) copy-start(s32[4]{0:T(128)} %start_ref.5) | copy-start | bytes 52
  18.1 14.1 %collective-permute-start.3 = (bf16[2,2,128,128]{3,2,1,0:T(8,128)(2,1)}, bf16[2,2,128,128]{3,2,1,0:T(8,128)(2,1)S(1)}, u32[]{:S(2)}, u32[]{:S(2)}) collective-permute-start(bf16[2,2,128,128]{3,2,1,0:T(8,128)(2,1)} %get-tuple-element.25), channel_id=1, source_target_pairs={{0,4},{4,0},{8,12},{12,8},{1,5},{5,1},{9,13},{13,9},{2,6},{6,2},{1... | collective-permute-start | bytes 393224 | tf_op jit(solution)/shard_map/ppermute | solution.py:270
  19.1 13.1 %collective-permute-start.4 = (bf16[2,2,128,128]{3,2,1,0:T(8,128)(2,1)}, bf16[2,2,128,128]{3,2,1,0:T(8,128)(2,1)S(1)}, u32[]{:S(2)}, u32[]{:S(2)}) collective-permute-start(bf16[2,2,128,128]{3,2,1,0:T(8,128)(2,1)} %get-tuple-element.26), channel_id=1, source_target_pairs={{0,8},{4,12},{8,0},{12,4},{1,9},{5,13},{9,1},{13,5},{2,10},{6,14},... | collective-permute-start | bytes 393224 | tf_op jit(solution)/shard_map/ppermute | solution.py:270
  22.5 9.6 %collective-permute-start.5 = (bf16[2,2,128,128]{3,2,1,0:T(8,128)(2,1)}, bf16[2,2,128,128]{3,2,1,0:T(8,128)(2,1)S(1)}, u32[]{:S(2)}, u32[]{:S(2)}) collective-permute-start(bf16[2,2,128,128]{3,2,1,0:T(8,128)(2,1)} %get-tuple-element.27), channel_id=1, source_target_pairs={{0,12},{4,8},{8,4},{12,0},{1,13},{5,9},{9,5},{13,1},{2,14},{6,10},... | collective-permute-start | bytes 393224 | tf_op jit(solution)/shard_map/ppermute | solution.py:270
  22.6 9.6 %copy-start = (bf16[2,2,128,128]{3,2,1,0:T(8,128)(2,1)S(1)}, bf16[2,2,128,128]{3,2,1,0:T(8,128)(2,1)}, u32[]{:S(2)}) copy-start(bf16[2,2,128,128]{3,2,1,0:T(8,128)(2,1)} %get-tuple-element.24.rest_0_) | copy-start | bytes 393220
  22.6 9.6 %copy-start.1 = (s32[4,4,2]{1,2,0:T(2,128)S(1)}, s32[4,4,2]{1,2,0:T(2,128)}, u32[]{:S(2)}) copy-start(s32[4,4,2]{1,2,0:T(2,128)} %param.11) | copy-start | bytes 388

commit v6 on v5

--- a/solution.py
+++ b/solution.py
@@ -281,7 +281,7 @@
     )(slot_of, pool_kv)
     received = exchange(sends)
 
-    per_step = math.gcd(per_kv, 4)
+    per_step = math.gcd(per_kv, 8)
     steps = per_kv // per_step
     scale = math.log2(math.e) / math.sqrt(head_dim)
 

time: 33.9 us -> 33.8 us (level)
  no operation moved by 1% of the time
where the time goes in v6:
time: 33.8 us; the launch traced here: 33.6 us
  Pallas kernels  22.7 us (67%)
  starting transfers between devices  10.1 us (30%)
  between operations  0.68 us (2%)
    ppermute x6, starting transfers between devices, exchange(): arrived[step - 1] = lax.ppermute(sends[step - 1], 'pool', pairs)  10.1 us
    pallas_call x1, Pallas kernels, body(): pl.pallas_call(functools.partial(prefix_kernel, scale, per_step), grid=(h...  9.52 us
    pallas_call x1, Pallas kernels, body(): pl.pallas_call(functools.partial(suffix_kernel, scale, per_kv), grid=(hea...  9.37 us
    pallas_call x1, Pallas kernels, body(): pl.pallas_call(fetch_kernel, out_shape=[pltpu.VMEM((fetched,) + page, dty...  2.39 us
    pallas_call x1, Pallas kernels, body(): pl.pallas_call(functools.partial(place_kernel, pages), out_shape=jax.Shap...  1.46 us
  transfers between devices with their start and end apart: 6, of which 0 were waited for; matrix products, arithmetic and copies ran while one was open for 0% of the time, Pallas kernels for 56%

profile of v6, /device:TPU:0, one launch (start us, length us, event | category | flops | bytes accessed | tf_op | source)
XLA Modules:
  0.0 33.6 jit_solution(10752845304022908615)
XLA Ops:
  0.6 2.4 %gather_pages.1 = (bf16[1,2,2,128,128]{4,3,2,1,0:T(8,128)(2,1)S(1)}, bf16[1,2,2,128,128]{4,3,2,1,0:T(8,128)(2,1)S(1)}, bf16[1,2,2,128,128]{4,3,2,1,0:T(8,128)(2,...) custom-call(s32[4,2,4]{2,1,0:T(2,128)} %bitcast.1, bf16[2,2,8,128,128]{4,3,2,1,0:T(8,128)(2,1)} %pool_ref.3), custom_call_target="tpu_custom_call" | custom-call | tf_op jit(solution)/shard_map/gather_pages/pallas_call | solution.py:273
  3.0 3.1 %collective-permute-start = (bf16[1,2,2,128,128]{4,3,2,1,0:T(8,128)(2,1)S(1)}, bf16[1,2,2,128,128]{4,3,2,1,0:T(8,128)(2,1)S(1)}, u32[]{:S(2)}, u32[]{:S(2)}) collective-permute-start(bf16[1,2,2,128,128]{4,3,2,1,0:T(8,128)(2,1)S(1)} %get-tuple-element.20), channel_id=1, source_target_pairs={{0,4},{4,0},{8,12},{12,8},{1,5},{5,1},{9,13},{13,9},{2,6},{6,2},{1... | collective-permute-start | bytes 393224 | tf_op jit(solution)/shard_map/ppermute | solution.py:270
  6.1 2.6 %collective-permute-start.1 = (bf16[1,2,2,128,128]{4,3,2,1,0:T(8,128)(2,1)S(1)}, bf16[1,2,2,128,128]{4,3,2,1,0:T(8,128)(2,1)S(1)}, u32[]{:S(2)}, u32[]{:S(2)}) collective-permute-start(bf16[1,2,2,128,128]{4,3,2,1,0:T(8,128)(2,1)S(1)} %get-tuple-element.21), channel_id=1, source_target_pairs={{0,8},{4,12},{8,0},{12,4},{1,9},{5,13},{9,1},{13,5},{2,10},{6,14},... | collective-permute-start | bytes 393224 | tf_op jit(solution)/shard_map/ppermute | solution.py:270
  8.7 0.0 collective-permute-start.2
  8.7 0.0 copy-start.2
  8.7 0.0 copy-start.3
  8.7 9.4 %attend_suffix.1 = (f32[2,8,512,128]{3,2,1,0:T(8,128)}, f32[2,8,512,128]{3,2,1,0:T(8,128)}, bf16[2,2,8,128,128]{4,3,2,1,0:T(8,128)(2,1)}, bf16[2,2,128,128]{3,2,...) custom-call(s32[4]{0:T(128)} %length_ref.5, ...), custom_call_target="tpu_custom_call" | custom-call | flops 3221225472 | bytes 8388608 | tf_op jit(solution)/shard_map/attend_suffix/pallas_call | solution.py:302
  18.1 1.0 %collective-permute-start.3 = (bf16[2,2,128,128]{3,2,1,0:T(8,128)(2,1)}, bf16[2,2,128,128]{3,2,1,0:T(8,128)(2,1)S(1)}, u32[]{:S(2)}, u32[]{:S(2)}) collective-permute-start(bf16[2,2,128,128]{3,2,1,0:T(8,128)(2,1)} %get-tuple-element.25), channel_id=1, source_target_pairs={{0,4},{4,0},{8,12},{12,8},{1,5},{5,1},{9,13},{13,9},{2,6},{6,2},{1... | collective-permute-start | bytes 393224 | tf_op jit(solution)/shard_map/ppermute | solution.py:270
  19.1 3.5 %collective-permute-start.4 = (bf16[2,2,128,128]{3,2,1,0:T(8,128)(2,1)}, bf16[2,2,128,128]{3,2,1,0:T(8,128)(2,1)S(1)}, u32[]{:S(2)}, u32[]{:S(2)}) collective-permute-start(bf16[2,2,128,128]{3,2,1,0:T(8,128)(2,1)} %get-tuple-element.26), channel_id=1, source_target_pairs={{0,8},{4,12},{8,0},{12,4},{1,9},{5,13},{9,1},{13,5},{2,10},{6,14},... | collective-permute-start | bytes 393224 | tf_op jit(solution)/shard_map/ppermute | solution.py:270
  22.5 0.0 collective-permute-done.rest_1_
  22.5 0.0 collective-permute-start.5
  22.5 0.0 collective-permute-done.1.rest_2_
  22.5 0.0 collective-permute-done.2.rest_3_
  22.6 0.0 copy-done.2
  22.6 0.0 copy-done.3
  22.6 0.0 copy-start
  22.6 0.0 copy-start.1
  22.6 9.5 %attend_prefix.1 = (bf16[512,2048]{1,0:T(8,128)(2,1)}, f32[8,128]{1,0:T(8,128)S(1)}) custom-call(s32[4]{0:T(128)S(1)} %copy-done.2, s32[4]{0:T(128)S(1)} %copy-done.3, bf16[512,2048]{1,0:T(8,128)(2,1)} %query_ref.3, f32[2,8,512,128]{3,2,1,0:T(8,128)} %get-tuple-element.17.mean_ref, f32[2,8,512,128]{3,2,1,0:T(8,128)} %get-tuple-element.18.log_ref, ...), custom_call_target="tpu_custom_call" | custom-call | flops 3221225472 | bytes 8388608 | tf_op jit(solution)/shard_map/attend_prefix/pallas_call | solution.py:334
  32.1 0.0 collective-permute-done.3.rest_1_
  32.1 0.0 collective-permute-done.4.rest_2_
  32.2 0.0 collective-permute-done.5.rest_3_
  32.2 0.0 copy-done
  32.2 0.0 copy-done.1
  32.2 1.5 %place_pages.1 = bf16[2,2,8,128,128]{4,3,2,1,0:T(8,128)(2,1)} custom-call(s32[4]{0:T(128)S(1)} %copy-done.2, s32[4]{0:T(128)S(1)} %copy-done.3, s32[4,2,4]{2,1,0:T(2,128)S(1)} %bitcast.2, bf16[2,2,128,128]{3,2,1,0:T(8,128)(2,1)S(1)} %copy-done, bf16[2,2,128,128]{3,2,1,0:T(8,128)(2,1)S(1)} %collective-permute-done.3.rest_1_, ...), custom_call_target="tpu_custom_call", output_to_operand_aliasing={{}: (8, {})} | custom-call | tf_op jit(solution)/shard_map/place_pages/pallas_call | solution.py:359
Async XLA Ops:
  3.0 19.5 %collective-permute-start = (bf16[1,2,2,128,128]{4,3,2,1,0:T(8,128)(2,1)S(1)}, bf16[1,2,2,128,128]{4,3,2,1,0:T(8,128)(2,1)S(1)}, u32[]{:S(2)}, u32[]{:S(2)}) collective-permute-start(bf16[1,2,2,128,128]{4,3,2,1,0:T(8,128)(2,1)S(1)} %get-tuple-element.20), channel_id=1, source_target_pairs={{0,4},{4,0},{8,12},{12,8},{1,5},{5,1},{9,13},{13,9},{2,6},{6,2},{1... | collective-permute-start | bytes 393224 | tf_op jit(solution)/shard_map/ppermute | solution.py:270
  6.1 16.4 %collective-permute-start.1 = (bf16[1,2,2,128,128]{4,3,2,1,0:T(8,128)(2,1)S(1)}, bf16[1,2,2,128,128]{4,3,2,1,0:T(8,128)(2,1)S(1)}, u32[]{:S(2)}, u32[]{:S(2)}) collective-permute-start(bf16[1,2,2,128,128]{4,3,2,1,0:T(8,128)(2,1)S(1)} %get-tuple-element.21), channel_id=1, source_target_pairs={{0,8},{4,12},{8,0},{12,4},{1,9},{5,13},{9,1},{13,5},{2,10},{6,14},... | collective-permute-start | bytes 393224 | tf_op jit(solution)/shard_map/ppermute | solution.py:270
  8.7 13.8 %collective-permute-start.2 = (bf16[1,2,2,128,128]{4,3,2,1,0:T(8,128)(2,1)S(1)}, bf16[1,2,2,128,128]{4,3,2,1,0:T(8,128)(2,1)S(1)}, u32[]{:S(2)}, u32[]{:S(2)}) collective-permute-start(bf16[1,2,2,128,128]{4,3,2,1,0:T(8,128)(2,1)S(1)} %get-tuple-element.22), channel_id=1, source_target_pairs={{0,12},{4,8},{8,4},{12,0},{1,13},{5,9},{9,5},{13,1},{2,14},{6,10},... | collective-permute-start | bytes 393224 | tf_op jit(solution)/shard_map/ppermute | solution.py:270
  8.7 13.8 %copy-start.2 = (s32[4]{0:T(128)S(1)}, s32[4]{0:T(128)}, u32[]{:S(2)}) copy-start(s32[4]{0:T(128)} %length_ref.5) | copy-start | bytes 52
  8.7 13.9 %copy-start.3 = (s32[4]{0:T(128)S(1)}, s32[4]{0:T(128)}, u32[]{:S(2)}) copy-start(s32[4]{0:T(128)} %start_ref.5) | copy-start | bytes 52
  18.1 14.0 %collective-permute-start.3 = (bf16[2,2,128,128]{3,2,1,0:T(8,128)(2,1)}, bf16[2,2,128,128]{3,2,1,0:T(8,128)(2,1)S(1)}, u32[]{:S(2)}, u32[]{:S(2)}) collective-permute-start(bf16[2,2,128,128]{3,2,1,0:T(8,128)(2,1)} %get-tuple-element.25), channel_id=1, source_target_pairs={{0,4},{4,0},{8,12},{12,8},{1,5},{5,1},{9,13},{13,9},{2,6},{6,2},{1... | collective-permute-start | bytes 393224 | tf_op jit(solution)/shard_map/ppermute | solution.py:270
  19.1 13.1 %collective-permute-start.4 = (bf16[2,2,128,128]{3,2,1,0:T(8,128)(2,1)}, bf16[2,2,128,128]{3,2,1,0:T(8,128)(2,1)S(1)}, u32[]{:S(2)}, u32[]{:S(2)}) collective-permute-start(bf16[2,2,128,128]{3,2,1,0:T(8,128)(2,1)} %get-tuple-element.26), channel_id=1, source_target_pairs={{0,8},{4,12},{8,0},{12,4},{1,9},{5,13},{9,1},{13,5},{2,10},{6,14},... | collective-permute-start | bytes 393224 | tf_op jit(solution)/shard_map/ppermute | solution.py:270
  22.5 9.6 %collective-permute-start.5 = (bf16[2,2,128,128]{3,2,1,0:T(8,128)(2,1)}, bf16[2,2,128,128]{3,2,1,0:T(8,128)(2,1)S(1)}, u32[]{:S(2)}, u32[]{:S(2)}) collective-permute-start(bf16[2,2,128,128]{3,2,1,0:T(8,128)(2,1)} %get-tuple-element.27), channel_id=1, source_target_pairs={{0,12},{4,8},{8,4},{12,0},{1,13},{5,9},{9,5},{13,1},{2,14},{6,10},... | collective-permute-start | bytes 393224 | tf_op jit(solution)/shard_map/ppermute | solution.py:270
  22.6 9.6 %copy-start = (bf16[2,2,128,128]{3,2,1,0:T(8,128)(2,1)S(1)}, bf16[2,2,128,128]{3,2,1,0:T(8,128)(2,1)}, u32[]{:S(2)}) copy-start(bf16[2,2,128,128]{3,2,1,0:T(8,128)(2,1)} %get-tuple-element.24.rest_0_) | copy-start | bytes 393220
  22.6 9.6 %copy-start.1 = (s32[4,4,2]{1,2,0:T(2,128)S(1)}, s32[4,4,2]{1,2,0:T(2,128)}, u32[]{:S(2)}) copy-start(s32[4,4,2]{1,2,0:T(2,128)} %param.11) | copy-start | bytes 388

commit v7 on v6

--- a/solution.py
+++ b/solution.py
@@ -149,12 +149,10 @@
         ]
         blocks = len(scores)
         tops = [
-            functools.reduce(
-                jnp.maximum,
-                [
-                    jnp.max(scores[key][row - key], axis=1, keepdims=True)
-                    for key in range(row + 1)
-                ],
+            jnp.max(
+                functools.reduce(jnp.maximum, [scores[key][row - key] for key in range(row + 1)]),
+                axis=1,
+                keepdims=True,
             )
             for row in range(blocks)
         ]

time: 33.8 us -> 33.7 us (level)
  no operation moved by 1% of the time
where the time goes in v7:
time: 33.7 us; the launch traced here: 33.5 us
  Pallas kernels  22.6 us (67%)
  starting transfers between devices  10.1 us (30%)
  between operations  0.69 us (2%)
    ppermute x6, starting transfers between devices, exchange(): arrived[step - 1] = lax.ppermute(sends[step - 1], 'pool', pairs)  10.1 us
    pallas_call x1, Pallas kernels, body(): pl.pallas_call(functools.partial(prefix_kernel, scale, per_step), grid=(h...  9.53 us
    pallas_call x1, Pallas kernels, body(): pl.pallas_call(functools.partial(suffix_kernel, scale, per_kv), grid=(hea...  9.2 us
    pallas_call x1, Pallas kernels, body(): pl.pallas_call(fetch_kernel, out_shape=[pltpu.VMEM((fetched,) + page, dty...  2.39 us
    pallas_call x1, Pallas kernels, body(): pl.pallas_call(functools.partial(place_kernel, pages), out_shape=jax.Shap...  1.46 us
  transfers between devices with their start and end apart: 6, of which 0 were waited for; matrix products, arithmetic and copies ran while one was open for 0% of the time, Pallas kernels for 56%

profile of v7, /device:TPU:0, one launch (start us, length us, event | category | flops | bytes accessed | tf_op | source)
XLA Modules:
  0.0 33.5 jit_solution(17021684385975443741)
XLA Ops:
  0.6 2.4 %gather_pages.1 = (bf16[1,2,2,128,128]{4,3,2,1,0:T(8,128)(2,1)S(1)}, bf16[1,2,2,128,128]{4,3,2,1,0:T(8,128)(2,1)S(1)}, bf16[1,2,2,128,128]{4,3,2,1,0:T(8,128)(2,...) custom-call(s32[4,2,4]{2,1,0:T(2,128)} %bitcast.1, bf16[2,2,8,128,128]{4,3,2,1,0:T(8,128)(2,1)} %pool_ref.3), custom_call_target="tpu_custom_call" | custom-call | tf_op jit(solution)/shard_map/gather_pages/pallas_call | solution.py:271
  3.0 3.1 %collective-permute-start = (bf16[1,2,2,128,128]{4,3,2,1,0:T(8,128)(2,1)S(1)}, bf16[1,2,2,128,128]{4,3,2,1,0:T(8,128)(2,1)S(1)}, u32[]{:S(2)}, u32[]{:S(2)}) collective-permute-start(bf16[1,2,2,128,128]{4,3,2,1,0:T(8,128)(2,1)S(1)} %get-tuple-element.20), channel_id=1, source_target_pairs={{0,4},{4,0},{8,12},{12,8},{1,5},{5,1},{9,13},{13,9},{2,6},{6,2},{1... | collective-permute-start | bytes 393224 | tf_op jit(solution)/shard_map/ppermute | solution.py:268
  6.1 2.6 %collective-permute-start.1 = (bf16[1,2,2,128,128]{4,3,2,1,0:T(8,128)(2,1)S(1)}, bf16[1,2,2,128,128]{4,3,2,1,0:T(8,128)(2,1)S(1)}, u32[]{:S(2)}, u32[]{:S(2)}) collective-permute-start(bf16[1,2,2,128,128]{4,3,2,1,0:T(8,128)(2,1)S(1)} %get-tuple-element.21), channel_id=1, source_target_pairs={{0,8},{4,12},{8,0},{12,4},{1,9},{5,13},{9,1},{13,5},{2,10},{6,14},... | collective-permute-start | bytes 393224 | tf_op jit(solution)/shard_map/ppermute | solution.py:268
  8.7 0.0 collective-permute-start.2
  8.7 0.0 copy-start.2
  8.7 0.0 copy-start.3
  8.7 9.2 %attend_suffix.1 = (f32[2,8,512,128]{3,2,1,0:T(8,128)}, f32[2,8,512,128]{3,2,1,0:T(8,128)}, bf16[2,2,8,128,128]{4,3,2,1,0:T(8,128)(2,1)}, bf16[2,2,128,128]{3,2,...) custom-call(s32[4]{0:T(128)} %length_ref.5, ...), custom_call_target="tpu_custom_call" | custom-call | flops 3221225472 | bytes 8388608 | tf_op jit(solution)/shard_map/attend_suffix/pallas_call | solution.py:300
  17.9 1.0 %collective-permute-start.3 = (bf16[2,2,128,128]{3,2,1,0:T(8,128)(2,1)}, bf16[2,2,128,128]{3,2,1,0:T(8,128)(2,1)S(1)}, u32[]{:S(2)}, u32[]{:S(2)}) collective-permute-start(bf16[2,2,128,128]{3,2,1,0:T(8,128)(2,1)} %get-tuple-element.25), channel_id=1, source_target_pairs={{0,4},{4,0},{8,12},{12,8},{1,5},{5,1},{9,13},{13,9},{2,6},{6,2},{1... | collective-permute-start | bytes 393224 | tf_op jit(solution)/shard_map/ppermute | solution.py:268
  18.9 3.5 %collective-permute-start.4 = (bf16[2,2,128,128]{3,2,1,0:T(8,128)(2,1)}, bf16[2,2,128,128]{3,2,1,0:T(8,128)(2,1)S(1)}, u32[]{:S(2)}, u32[]{:S(2)}) collective-permute-start(bf16[2,2,128,128]{3,2,1,0:T(8,128)(2,1)} %get-tuple-element.26), channel_id=1, source_target_pairs={{0,8},{4,12},{8,0},{12,4},{1,9},{5,13},{9,1},{13,5},{2,10},{6,14},... | collective-permute-start | bytes 393224 | tf_op jit(solution)/shard_map/ppermute | solution.py:268
  22.4 0.0 collective-permute-done.rest_1_
  22.4 0.0 collective-permute-start.5
  22.4 0.0 collective-permute-done.1.rest_2_
  22.4 0.0 collective-permute-done.2.rest_3_
  22.4 0.0 copy-done.2
  22.4 0.0 copy-done.3
  22.4 0.0 copy-start
  22.4 0.0 copy-start.1
  22.4 9.5 %attend_prefix.1 = (bf16[512,2048]{1,0:T(8,128)(2,1)}, f32[8,128]{1,0:T(8,128)S(1)}) custom-call(s32[4]{0:T(128)S(1)} %copy-done.2, s32[4]{0:T(128)S(1)} %copy-done.3, bf16[512,2048]{1,0:T(8,128)(2,1)} %query_ref.3, f32[2,8,512,128]{3,2,1,0:T(8,128)} %get-tuple-element.17.mean_ref, f32[2,8,512,128]{3,2,1,0:T(8,128)} %get-tuple-element.18.log_ref, ...), custom_call_target="tpu_custom_call" | custom-call | flops 3221225472 | bytes 8388608 | tf_op jit(solution)/shard_map/attend_prefix/pallas_call | solution.py:332
  32.0 0.0 collective-permute-done.3.rest_1_
  32.0 0.0 collective-permute-done.4.rest_2_
  32.0 0.0 collective-permute-done.5.rest_3_
  32.0 0.0 copy-done
  32.0 0.0 copy-done.1
  32.0 1.5 %place_pages.1 = bf16[2,2,8,128,128]{4,3,2,1,0:T(8,128)(2,1)} custom-call(s32[4]{0:T(128)S(1)} %copy-done.2, s32[4]{0:T(128)S(1)} %copy-done.3, s32[4,2,4]{2,1,0:T(2,128)S(1)} %bitcast.2, bf16[2,2,128,128]{3,2,1,0:T(8,128)(2,1)S(1)} %copy-done, bf16[2,2,128,128]{3,2,1,0:T(8,128)(2,1)S(1)} %collective-permute-done.3.rest_1_, ...), custom_call_target="tpu_custom_call", output_to_operand_aliasing={{}: (8, {})} | custom-call | tf_op jit(solution)/shard_map/place_pages/pallas_call | solution.py:357
Async XLA Ops:
  3.0 19.3 %collective-permute-start = (bf16[1,2,2,128,128]{4,3,2,1,0:T(8,128)(2,1)S(1)}, bf16[1,2,2,128,128]{4,3,2,1,0:T(8,128)(2,1)S(1)}, u32[]{:S(2)}, u32[]{:S(2)}) collective-permute-start(bf16[1,2,2,128,128]{4,3,2,1,0:T(8,128)(2,1)S(1)} %get-tuple-element.20), channel_id=1, source_target_pairs={{0,4},{4,0},{8,12},{12,8},{1,5},{5,1},{9,13},{13,9},{2,6},{6,2},{1... | collective-permute-start | bytes 393224 | tf_op jit(solution)/shard_map/ppermute | solution.py:268
  6.1 16.3 %collective-permute-start.1 = (bf16[1,2,2,128,128]{4,3,2,1,0:T(8,128)(2,1)S(1)}, bf16[1,2,2,128,128]{4,3,2,1,0:T(8,128)(2,1)S(1)}, u32[]{:S(2)}, u32[]{:S(2)}) collective-permute-start(bf16[1,2,2,128,128]{4,3,2,1,0:T(8,128)(2,1)S(1)} %get-tuple-element.21), channel_id=1, source_target_pairs={{0,8},{4,12},{8,0},{12,4},{1,9},{5,13},{9,1},{13,5},{2,10},{6,14},... | collective-permute-start | bytes 393224 | tf_op jit(solution)/shard_map/ppermute | solution.py:268
  8.7 13.7 %collective-permute-start.2 = (bf16[1,2,2,128,128]{4,3,2,1,0:T(8,128)(2,1)S(1)}, bf16[1,2,2,128,128]{4,3,2,1,0:T(8,128)(2,1)S(1)}, u32[]{:S(2)}, u32[]{:S(2)}) collective-permute-start(bf16[1,2,2,128,128]{4,3,2,1,0:T(8,128)(2,1)S(1)} %get-tuple-element.22), channel_id=1, source_target_pairs={{0,12},{4,8},{8,4},{12,0},{1,13},{5,9},{9,5},{13,1},{2,14},{6,10},... | collective-permute-start | bytes 393224 | tf_op jit(solution)/shard_map/ppermute | solution.py:268
  8.7 13.7 %copy-start.2 = (s32[4]{0:T(128)S(1)}, s32[4]{0:T(128)}, u32[]{:S(2)}) copy-start(s32[4]{0:T(128)} %length_ref.5) | copy-start | bytes 52
  8.7 13.7 %copy-start.3 = (s32[4]{0:T(128)S(1)}, s32[4]{0:T(128)}, u32[]{:S(2)}) copy-start(s32[4]{0:T(128)} %start_ref.5) | copy-start | bytes 52
  17.9 14.0 %collective-permute-start.3 = (bf16[2,2,128,128]{3,2,1,0:T(8,128)(2,1)}, bf16[2,2,128,128]{3,2,1,0:T(8,128)(2,1)S(1)}, u32[]{:S(2)}, u32[]{:S(2)}) collective-permute-start(bf16[2,2,128,128]{3,2,1,0:T(8,128)(2,1)} %get-tuple-element.25), channel_id=1, source_target_pairs={{0,4},{4,0},{8,12},{12,8},{1,5},{5,1},{9,13},{13,9},{2,6},{6,2},{1... | collective-permute-start | bytes 393224 | tf_op jit(solution)/shard_map/ppermute | solution.py:268
  18.9 13.1 %collective-permute-start.4 = (bf16[2,2,128,128]{3,2,1,0:T(8,128)(2,1)}, bf16[2,2,128,128]{3,2,1,0:T(8,128)(2,1)S(1)}, u32[]{:S(2)}, u32[]{:S(2)}) collective-permute-start(bf16[2,2,128,128]{3,2,1,0:T(8,128)(2,1)} %get-tuple-element.26), channel_id=1, source_target_pairs={{0,8},{4,12},{8,0},{12,4},{1,9},{5,13},{9,1},{13,5},{2,10},{6,14},... | collective-permute-start | bytes 393224 | tf_op jit(solution)/shard_map/ppermute | solution.py:268
  22.4 9.6 %collective-permute-start.5 = (bf16[2,2,128,128]{3,2,1,0:T(8,128)(2,1)}, bf16[2,2,128,128]{3,2,1,0:T(8,128)(2,1)S(1)}, u32[]{:S(2)}, u32[]{:S(2)}) collective-permute-start(bf16[2,2,128,128]{3,2,1,0:T(8,128)(2,1)} %get-tuple-element.27), channel_id=1, source_target_pairs={{0,12},{4,8},{8,4},{12,0},{1,13},{5,9},{9,5},{13,1},{2,14},{6,10},... | collective-permute-start | bytes 393224 | tf_op jit(solution)/shard_map/ppermute | solution.py:268
  22.4 9.6 %copy-start = (bf16[2,2,128,128]{3,2,1,0:T(8,128)(2,1)S(1)}, bf16[2,2,128,128]{3,2,1,0:T(8,128)(2,1)}, u32[]{:S(2)}) copy-start(bf16[2,2,128,128]{3,2,1,0:T(8,128)(2,1)} %get-tuple-element.24.rest_0_) | copy-start | bytes 393220
  22.4 9.6 %copy-start.1 = (s32[4,4,2]{1,2,0:T(2,128)S(1)}, s32[4,4,2]{1,2,0:T(2,128)}, u32[]{:S(2)}) copy-start(s32[4,4,2]{1,2,0:T(2,128)} %param.11) | copy-start | bytes 388
